TPU v7x, 32 devices: a whole 2x2x4 slice. The times are simulated.
32 devices in a mesh: fsdp: 4 (over y, core), ctx: 8 (over z, x).
Axes of the slice: x: 2, y: 2, z: 4, core: 2. Of those that a mesh axis runs over, the one named last changes fastest.
Arguments:
- tokens: bfloat16 [8, 1024, 2048], P('fsdp', 'ctx'), may hold values from -6 to 6
- lengths: int32 [8], P('fsdp'), may hold values from 1024 to 1024, as said below
- cotangent: bfloat16 [8, 1024, 2048], P('fsdp', 'ctx'), may hold values from -6 to 6
- norm_gain: bfloat16 [2048], P('fsdp'), may hold values from 0.5 to 1.5
- norm_shift: bfloat16 [2048], P('fsdp'), may hold values from -1.75 to 1.75
- query_weight: bfloat16 [2048, 2048], P('fsdp'), may hold values from -0.125 to 0.125
- query_bias: bfloat16 [2048], P('fsdp'), may hold values from -3 to 3
- keyval_weight: bfloat16 [2048, 256], P('fsdp'), may hold values from -0.125 to 0.125
- value_bias: bfloat16 [128], P('fsdp'), may hold values from -0.3125 to 0.3125
- mixer_weight: bfloat16 [2048, 2048], P('fsdp'), may hold values from -0.5 to 0.5
- mixer_bias: bfloat16 [2048], P('fsdp'), may hold values from -1.75 to 1.75
- ffnorm_gain: bfloat16 [2048], P('fsdp'), may hold values from 0.5 to 1.5
- ffnorm_shift: bfloat16 [2048], P('fsdp'), may hold values from -1.75 to 1.75
- up_weight: bfloat16 [2048, 8192], P('fsdp'), may hold values from -0.125 to 0.125
- up_bias: bfloat16 [8192], P('fsdp'), may hold values from -3 to 3
- down_weight: bfloat16 [8192, 2048], P('fsdp'), may hold values from -0.0625 to 0.0625
- down_bias: bfloat16 [2048], P('fsdp'), may hold values from -1.75 to 1.75
Outputs:
- layer_out: bfloat16 [8, 1024, 2048], P('fsdp', 'ctx')
- tokens_grad: bfloat16 [8, 1024, 2048], P('fsdp', 'ctx')
- gain_grad: float32 [2048], P(('fsdp', 'ctx'))
- shift_grad: float32 [2048], P(('fsdp', 'ctx'))
- query_grad: float32 [2048, 2048], P(('fsdp', 'ctx'))
- qbias_grad: float32 [2048], P(('fsdp', 'ctx'))
- keyval_grad: float32 [2048, 256], P(('fsdp', 'ctx'))
- vbias_grad: float32 [128], P(('fsdp', 'ctx'))
- mixer_grad: float32 [2048, 2048], P(('fsdp', 'ctx'))
- mbias_grad: float32 [2048], P(('fsdp', 'ctx'))
- ffgain_grad: float32 [2048], P(('fsdp', 'ctx'))
- ffshift_grad: float32 [2048], P(('fsdp', 'ctx'))
- up_grad: float32 [2048, 8192], P(('fsdp', 'ctx'))
- ubias_grad: float32 [8192], P(('fsdp', 'ctx'))
- down_grad: float32 [8192, 2048], P(('fsdp', 'ctx'))
- dbias_grad: float32 [2048], P(('fsdp', 'ctx'))
Inputs may be any that keep to these rules, and one draw needn't show every extreme that they name: Slot s holds one sequence in its first lengths[s] positions and padding after it; of the 2 slots of each index of fsdp, one is full.
All inputs are finite; a program needn't handle non-finite values.
Results may differ from a plain program's by a relative error of at most 0.015.
Values may be sent and summed in bfloat16 or wider, within the bound.
A program may use at most 384 MiB of HBM per device.

v0:
```python
import functools

import jax
import jax.numpy as jnp
from jax import lax
from jax.experimental import pallas as pl
from jax.experimental.pallas import tpu as pltpu
from jax.sharding import Mesh, PartitionSpec as P

EPSILON = 1e-05
NEG_LARGE = -1e30
MIN_LEN = 1024
BF = jnp.bfloat16
F32 = jnp.float32
GELU_K = 0.7978845608028654
GELU_C = 0.044715


def dot(left_side, right_side, dims=((1,), (0,))):
    return lax.dot_general(left_side, right_side, (dims, ((), ())), preferred_element_type=F32)


def swap(values, axis):
    return lax.ppermute(values, axis, [(0, 1), (1, 0)])


def pick(values, index, axis):
    return lax.dynamic_index_in_dim(values, index, axis, keepdims=False)


def stack_heads(block, head_dim):
    heads = block.shape[0] // head_dim
    return jnp.concatenate([block[h * head_dim : (h + 1) * head_dim] for h in range(heads)], axis=1)


def unstack_heads(stacked, seg):
    heads = stacked.shape[1] // seg
    return jnp.concatenate([stacked[:, h * seg : (h + 1) * seg] for h in range(heads)], axis=0)


def masked_scores(scal_ref, queries, keys, step, seg, heads, with_length, first_block):
    scores = dot(keys, queries) * (keys.shape[1] ** (-0.5))
    pair = keys.shape[0]
    if not (with_length or first_block):
        return scores
    key_pos = lax.broadcasted_iota(jnp.int32, (pair, seg), 0)
    allowed = None
    if first_block:
        query_pos = lax.broadcasted_iota(jnp.int32, (pair, seg), 1) + scal_ref[1] * seg
        allowed = key_pos <= query_pos
    if with_length:
        length = scal_ref[2 + pl.program_id(0)]
        inside = key_pos + (scal_ref[0] - step) * pair < length
        allowed = inside if allowed is None else allowed & inside
    bias = jnp.where(allowed, 0.0, NEG_LARGE).astype(F32)
    return scores + jnp.concatenate([bias] * heads, axis=1)


def attn_fwd_kernel(scal_ref, q_ref, kv_ref, out_ref, lse_ref, *, with_length):
    head_dim = kv_ref.shape[-1] // 2
    seg = q_ref.shape[1]
    heads = q_ref.shape[0] // head_dim
    queries = stack_heads(q_ref[...], head_dim)

    def block(step, state, first_block):
        top, total, accum = state
        keys = kv_ref[0, step, :, :head_dim]
        values = kv_ref[0, step, :, head_dim:]
        scores = masked_scores(scal_ref, queries, keys, step, seg, heads, with_length, first_block)
        new_top = jnp.maximum(top, jnp.max(scores, axis=0, keepdims=True))
        terms = jnp.exp(scores - new_top)
        fade = jnp.exp(top - new_top)
        total = total * fade + jnp.sum(terms, axis=0, keepdims=True)
        accum = accum * fade + dot(values, terms.astype(BF), ((0,), (0,)))
        return new_top, total, accum

    lanes = heads * seg
    state = (
        jnp.full((1, lanes), NEG_LARGE, F32),
        jnp.zeros((1, lanes), F32),
        jnp.zeros((head_dim, lanes), F32),
    )
    state = block(0, state, True)
    top, total, accum = lax.fori_loop(1, scal_ref[0] + 1, lambda t, s: block(t, s, False), state)
    out_ref[...] = unstack_heads(accum / total, seg).astype(BF)
    lse_ref[0, 0] = top + jnp.log(total)


def attn_bwd_kernel(scal_ref, q_ref, kv_ref, out_ref, dout_ref, lse_ref, dq_ref, dkv_ref, *, with_length):
    head_dim = kv_ref.shape[-1] // 2
    seg = q_ref.shape[1]
    heads = q_ref.shape[0] // head_dim
    scale = head_dim ** (-0.5)
    queries = stack_heads(q_ref[...], head_dim)
    d_mixed = stack_heads(dout_ref[...], head_dim)
    mixed = stack_heads(out_ref[...], head_dim)
    delta = jnp.sum(mixed.astype(F32) * d_mixed.astype(F32), axis=0, keepdims=True)
    lse = lse_ref[0, 0]

    @pl.when(pl.program_id(1) == 0)
    def clear():
        dkv_ref[...] = jnp.zeros_like(dkv_ref)

    def block(step, accum, first_block):
        keys = kv_ref[0, step, :, :head_dim]
        values = kv_ref[0, step, :, head_dim:]
        scores = masked_scores(scal_ref, queries, keys, step, seg, heads, with_length, first_block)
        probs = jnp.exp(scores - lse)
        d_probs = dot(values, d_mixed)
        d_scores = (probs * (d_probs - delta)).astype(BF)
        dkv_ref[0, step, :, :head_dim] += dot(d_scores, queries, ((1,), (1,))) * scale
        dkv_ref[0, step, :, head_dim:] += dot(probs.astype(BF), d_mixed, ((1,), (1,)))
        return accum + dot(keys, d_scores, ((0,), (0,)))

    accum = block(0, jnp.zeros((head_dim, heads * seg), F32), True)
    accum = lax.fori_loop(1, scal_ref[0] + 1, lambda t, s: block(t, s, False), accum)
    dq_ref[...] = (unstack_heads(accum, seg) * scale).astype(BF)


def attn_specs(slots, steps, pair, seg, rows, groups, head_dim):
    lanes = rows // groups // head_dim * seg
    scal = pl.BlockSpec(memory_space=pltpu.SMEM)
    feat = pl.BlockSpec((rows // groups, seg), lambda s, g: (g, s))
    kv = pl.BlockSpec((1, steps, pair, 2 * head_dim), lambda s, g: (s, 0, 0, 0))
    lse = pl.BlockSpec((1, 1, 1, lanes), lambda s, g: (s, g, 0, 0))
    return scal, feat, kv, lse, lanes


def attn_forward(scal, q_t, kv, groups, with_length):
    slots, steps, pair, width = kv.shape
    rows, cols = q_t.shape
    seg = cols // slots
    scal_s, feat, kv_s, lse_s, lanes = attn_specs(slots, steps, pair, seg, rows, groups, width // 2)
    return pl.pallas_call(
        functools.partial(attn_fwd_kernel, with_length=with_length),
        grid=(slots, groups),
        in_specs=[scal_s, feat, kv_s],
        out_specs=[feat, lse_s],
        out_shape=[
            jax.ShapeDtypeStruct((rows, cols), BF),
            jax.ShapeDtypeStruct((slots, groups, 1, lanes), F32),
        ],
        compiler_params=pltpu.CompilerParams(vmem_limit_bytes=40 << 20),
        cost_estimate=pl.CostEstimate(
            flops=4 * rows * cols * steps * pair, bytes_accessed=6 << 20, transcendentals=0
        ),
    )(scal, q_t, kv)


def attn_backward(scal, q_t, kv, out_t, dout_t, lse, groups, with_length):
    slots, steps, pair, width = kv.shape
    rows, cols = q_t.shape
    seg = cols // slots
    scal_s, feat, kv_s, lse_s, lanes = attn_specs(slots, steps, pair, seg, rows, groups, width // 2)
    return pl.pallas_call(
        functools.partial(attn_bwd_kernel, with_length=with_length),
        grid=(slots, groups),
        in_specs=[scal_s, feat, kv_s, feat, feat, lse_s],
        out_specs=[feat, kv_s],
        out_shape=[
            jax.ShapeDtypeStruct((rows, cols), BF),
            jax.ShapeDtypeStruct(kv.shape, F32),
        ],
        compiler_params=pltpu.CompilerParams(vmem_limit_bytes=48 << 20),
        cost_estimate=pl.CostEstimate(
            flops=10 * rows * cols * steps * pair, bytes_accessed=9 << 20, transcendentals=0
        ),
    )(scal, q_t, kv, out_t, dout_t, lse)


def norm_stats(values):
    center = values - jnp.mean(values, axis=-1, keepdims=True)
    spread = jnp.mean(center * center, axis=-1, keepdims=True)
    rstd = lax.rsqrt(spread + EPSILON)
    return center * rstd, rstd


def norm_backward(d_values, unit, rstd, gain):
    scaled = d_values * gain
    return rstd * (
        scaled
        - jnp.mean(scaled, axis=-1, keepdims=True)
        - unit * jnp.mean(scaled * unit, axis=-1, keepdims=True)
    )


def gather_rows(shard, x, place):
    rows = shard.shape[0]
    half = rows // 2
    mine = lax.dynamic_slice_in_dim(shard, x * half, half, 0)
    direct = swap(mine, "y")
    other = swap(direct, "x")
    sib = swap(shard, "c")
    sib_direct = swap(direct, "c")
    sib_other = swap(other, "c")
    full = jnp.zeros((4 * rows,) + shard.shape[1:], shard.dtype)
    far = place ^ 2
    pieces = (
        (shard, place * rows),
        (sib, (place ^ 1) * rows),
        (direct, far * rows + x * half),
        (other, far * rows + (1 - x) * half),
        (sib_direct, (far ^ 1) * rows + x * half),
        (sib_other, (far ^ 1) * rows + (1 - x) * half),
    )
    for piece, start in pieces:
        full = lax.dynamic_update_slice_in_dim(full, piece, start, 0)
    return full


def gather_plane(block):
    half = block.shape[0] // 2
    from_x = swap(block, "x")
    from_y = swap(block, "y")
    diag = jnp.concatenate([swap(from_y[:half], "x"), swap(from_x[half:], "y")], axis=0)
    return [
        jnp.concatenate([part, swap(part, "c")], axis=0) for part in (block, from_x, from_y, diag)
    ]


def scatter_plane(parts):
    rows = parts[0].shape[0] // 2
    half = rows // 2
    own, to_x, to_y, diag = [
        part[:rows].astype(F32) + swap(part[rows:].astype(BF), "c").astype(F32) for part in parts
    ]
    via_x = swap(diag[:half].astype(BF), "x").astype(F32)
    via_y = swap(diag[half:].astype(BF), "y").astype(F32)
    to_y = jnp.concatenate([to_y[:half] + via_x, to_y[half:]], axis=0)
    to_x = jnp.concatenate([to_x[:half], to_x[half:] + via_y], axis=0)
    return own + swap(to_x.astype(BF), "x").astype(F32) + swap(to_y.astype(BF), "y").astype(F32)


def scatter_line(parts, z, length):
    def block(index):
        return pick(parts, jnp.clip(index, 0, length - 1), 0).astype(F32)

    from_left = from_right = None
    for step in range(1, length):
        up = block(length - step + z)
        down = block(z - length + step)
        if from_left is not None:
            up, down = up + from_left, down + from_right
        from_left = lax.ppermute(up.astype(BF), "z", [(i, i + 1) for i in range(step)]).astype(F32)
        from_right = lax.ppermute(
            down.astype(BF), "z", [(i, i - 1) for i in range(length - step, length)]
        ).astype(F32)
    return block(z) + from_left + from_right


def scatter_all(left_side, right_side, vectors, place_yczx, sizes):
    y, c, z, x = place_yczx
    length, width = sizes
    tokens = left_side.shape[0]
    block = width // (8 * length)
    left_parts = left_side.reshape(tokens, 2, 2, width // 4)
    left_mine = pick(left_parts, c, 2).reshape(tokens, width // 2)
    left_sib = swap(pick(left_parts, 1 - c, 2), "c").reshape(tokens, width // 2)
    right_sib = swap(right_side, "c")
    partial = dot(
        jnp.concatenate([left_mine, left_sib], axis=0),
        jnp.concatenate([right_side, right_sib], axis=0),
        ((0,), (0,)),
    )
    extra = jnp.pad(jnp.stack(vectors, axis=1), ((0, 0), (0, 128 - len(vectors))))
    extra = extra.reshape(2, 2, width // 4, 128)
    extra = pick(extra, c, 1) + swap(pick(extra, 1 - c, 1).astype(BF), "c").astype(F32)
    partial = jnp.concatenate([partial, extra.reshape(width // 2, 128)], axis=1)
    cols = partial.shape[1]
    partial = partial.reshape(2, length, 2, block, cols)
    cut = (cols // 256) * 128
    side_a, side_b = partial[..., :cut], partial[..., cut:]
    side_a = pick(side_a, y, 0) + swap(pick(side_a, 1 - y, 0).astype(BF), "y").astype(F32)
    side_b = pick(side_b, x, 2) + swap(pick(side_b, 1 - x, 2).astype(BF), "x").astype(F32)
    side_a = pick(side_a, x, 1) + swap(pick(side_a, 1 - x, 1).astype(BF), "x").astype(F32)
    side_b = pick(side_b, y, 0) + swap(pick(side_b, 1 - y, 0).astype(BF), "y").astype(F32)
    return scatter_line(jnp.concatenate([side_a, side_b], axis=-1), z, length)


MESH = pl.DeviceIdType.MESH


def remote(src, dst, send_sems, recv_sems, index, device):
    return pltpu.make_async_remote_copy(
        src_ref=src,
        dst_ref=dst,
        send_sem=send_sems.at[index],
        recv_sem=recv_sems.at[index],
        device_id=device,
        device_id_type=MESH,
    )


def greet(devices):
    barrier = pltpu.get_barrier_semaphore()
    for device in devices:
        pl.semaphore_signal(barrier, inc=1, device_id=device, device_id_type=MESH)
    pl.semaphore_wait(barrier, len(devices))


def tiles(count, size):
    def over(fn):
        @pl.loop(0, count)
        def step(index):
            fn(pl.ds(pl.multiple_of(index * size, size), size), index)

    return over


def gelu_pair(upper):
    inner = jnp.tanh(upper * (GELU_K + (GELU_K * GELU_C) * (upper * upper)))
    half = 0.5 + 0.5 * inner
    slope = half + (0.5 * upper) * (1.0 - inner * inner) * (
        GELU_K + (3.0 * GELU_K * GELU_C) * (upper * upper)
    )
    return upper * half, slope


def ffn_kernel(
    second_ref,
    down_all_ref,
    up_ref,
    ubias_ref,
    down_ref,
    dsecond_ref,
    out_parts_ref,
    down_part_ref,
    up_part_ref,
    ubias_part_ref,
    tokens_v,
    cots_v,
    up_v,
    down_v,
    active_v,
    dupper_v,
    sib_out,
    sib_in,
    chip_out,
    chip_in,
    acc_v,
    stage_v,
    load_sem,
    stage_sem,
    gs_send,
    gs_recv,
    rs_send,
    rs_recv,
    *,
    length,
):
    rows, width = second_ref.shape
    hidden = up_ref.shape[1]
    half = rows // 2
    chunk = 2 * rows
    y, c, x = [lax.axis_index(name) for name in ("y", "c", "x")]
    sib, to_x, to_y = {"c": 1 - c}, {"x": 1 - x}, {"y": 1 - y}
    diag = {"x": 1 - x, "y": 1 - y}
    chips = (None, to_x, to_y, diag)

    loads = [
        pltpu.make_async_copy(second_ref, tokens_v.at[0, pl.ds(0, rows)], load_sem.at[0]),
        pltpu.make_async_copy(down_ref, down_v, load_sem.at[1]),
        pltpu.make_async_copy(down_all_ref, cots_v, load_sem.at[2]),
        pltpu.make_async_copy(up_ref, up_v, load_sem.at[3]),
    ]
    for load in loads:
        load.start()
    greet((sib, to_x, to_y, diag))
    loads[0].wait()

    same, other = pl.ds(0, rows), pl.ds(rows, rows)
    top, bottom = pl.ds(0, half), pl.ds(half, half)

    def gather(index, chip, span_src, chip_dst, span_dst, device):
        return remote(
            tokens_v.at[chip, span_src], tokens_v.at[chip_dst, span_dst], gs_send, gs_recv, index, device
        )

    send_x = gather(0, 0, same, 1, same, to_x)
    send_y = gather(1, 0, same, 2, same, to_y)
    share = [gather(2 + k, k, same, k, other, sib) for k in range(4)]
    diag_x = gather(6, 2, top, 3, top, to_x)
    diag_y = gather(7, 1, bottom, 3, bottom, to_y)
    send_x.start()
    send_y.start()
    share[0].start()

    loads[1].wait()
    loads[2].wait()

    @tiles(4 * chunk // 512, 512)
    def grad_active(span, index):
        @tiles(hidden // 512, 512)
        def columns(cols, _):
            dupper_v[span, cols] = dot(cots_v[span, :], down_v[cols, :], ((1,), (1,))).astype(BF)

    loads[3].wait()

    def chip_work(k):
        @tiles(hidden // 256, 256)
        def columns(cols, _):
            block = pl.ds(k * chunk, chunk)
            upper = dot(tokens_v[k], up_v[:, cols]) + ubias_ref[:, cols]
            active, slope = gelu_pair(upper)
            active_v[block, cols] = active.astype(BF)
            d_upper = (dupper_v[block, cols].astype(F32) * slope).astype(BF)
            dupper_v[block, cols] = d_upper
            part = jnp.sum(d_upper.astype(F32), axis=0, keepdims=True)
            if k == 0:
                ubias_part_ref[:, cols] = part
            else:
                ubias_part_ref[:, cols] += part

        @tiles(width // 512, 512)
        def to_sibling(cols, _):
            sib_out[k, :, cols] = dot(
                dupper_v[pl.ds(k * chunk + rows, rows), :], up_v[cols, :], ((1,), (1,))
            ).astype(BF)

        pair = remote(sib_out.at[k], sib_in.at[k], rs_send, rs_recv, k, sib)
        pair.start()

        @tiles(width // 512, 512)
        def keep(cols, _):
            acc_v[:, cols] = dot(dupper_v[pl.ds(k * chunk, rows), :], up_v[cols, :], ((1,), (1,)))

        pair.wait_recv()
        if k == 0:
            dsecond_ref[...] = acc_v[...] + sib_in[0].astype(F32)
            return [pair]
        chip_out[k - 1] = (acc_v[...] + sib_in[k].astype(F32)).astype(BF)
        far = remote(chip_out.at[k - 1], chip_in.at[k - 1], rs_send, rs_recv, 3 + k, chips[k])
        far.start()
        return [pair, far]

    share[0].wait_recv()
    sent = chip_work(0)
    send_x.wait_recv()
    share[1].start()
    diag_y.start()
    send_y.wait_recv()
    share[2].start()
    diag_x.start()
    share[1].wait_recv()
    sent += chip_work(1)
    share[2].wait_recv()
    sent += chip_work(2)
    diag_x.wait_recv()
    diag_y.wait_recv()
    share[3].start()
    share[3].wait_recv()
    sent += chip_work(3)

    def staged(slot, value, target):
        stage_v[slot] = value.astype(BF)
        copy = pltpu.make_async_copy(stage_v.at[slot], target, stage_sem.at[slot])
        copy.start()
        return copy

    @pl.loop(0, 4)
    def outputs(k):
        block = pl.ds(pl.multiple_of(k * chunk, chunk), chunk)
        copies = []
        for j in range(width // 512):
            cols = pl.ds(j * 512, 512)
            copies.append(
                staged(j, dot(active_v[block, :], down_v[:, cols]), out_parts_ref.at[k, :, cols])
            )
        for copy in copies:
            copy.wait()

    @pl.loop(0, hidden // 512)
    def downs(r):
        block = pl.ds(pl.multiple_of(r * 512, 512), 512)
        copies = []
        for j in range(width // 512):
            cols = pl.ds(j * 512, 512)
            copies.append(
                staged(
                    j,
                    dot(active_v[:, block], cots_v[:, cols], ((0,), (0,))),
                    down_part_ref.at[block, cols],
                )
            )
        for copy in copies:
            copy.wait()

    quarter = width // 4
    piece = quarter // length

    @pl.loop(0, hidden // 512)
    def ups(r):
        cols = pl.ds(pl.multiple_of(r * 512, 512), 512)
        copies = []
        for f in range(4):
            value = None
            for k in range(4):
                term = dot(
                    tokens_v[k, :, f * quarter : (f + 1) * quarter],
                    dupper_v[k * chunk : (k + 1) * chunk, cols],
                    ((0,), (0,)),
                )
                value = term if value is None else value + term
            stage_v[f] = value.astype(BF)
            for level in range(length):
                copy = pltpu.make_async_copy(
                    stage_v.at[f, pl.ds(level * piece, piece)],
                    up_part_ref.at[level, f, :, cols],
                    stage_sem.at[4 + f * length + level],
                )
                copy.start()
                copies.append(copy)
        for copy in copies:
            copy.wait()

    for k in range(3):
        remote(chip_out.at[k], chip_in.at[k], rs_send, rs_recv, 4 + k, chips[k + 1]).wait_recv()
    dsecond_ref[...] += (
        chip_in[0].astype(F32) + chip_in[1].astype(F32) + chip_in[2].astype(F32)
    )
    for copy in [send_x, send_y, diag_x, diag_y] + share + sent:
        copy.wait_send()


def ffn(second, down_all, up_mine, ubias, down_mine, length):
    rows, width = second.shape
    hidden = up_mine.shape[1]
    hbm = pl.BlockSpec(memory_space=pltpu.HBM)
    vmem = pl.BlockSpec(memory_space=pltpu.VMEM)
    sems = pltpu.SemaphoreType.DMA
    return pl.pallas_call(
        functools.partial(ffn_kernel, length=length),
        in_specs=[hbm, hbm, hbm, vmem, hbm],
        out_specs=[vmem, hbm, hbm, hbm, vmem],
        out_shape=[
            jax.ShapeDtypeStruct((rows, width), F32),
            jax.ShapeDtypeStruct((4, 2 * rows, width), BF),
            jax.ShapeDtypeStruct((hidden, width), BF),
            jax.ShapeDtypeStruct((length, 4, width // 4 // length, hidden), BF),
            jax.ShapeDtypeStruct((1, hidden), F32),
        ],
        scratch_shapes=[
            pltpu.VMEM((4, 2 * rows, width), BF),
            pltpu.VMEM((8 * rows, width), BF),
            pltpu.VMEM((width, hidden), BF),
            pltpu.VMEM((hidden, width), BF),
            pltpu.VMEM((8 * rows, hidden), BF),
            pltpu.VMEM((8 * rows, hidden), BF),
            pltpu.VMEM((4, rows, width), BF),
            pltpu.VMEM((4, rows, width), BF),
            pltpu.VMEM((3, rows, width), BF),
            pltpu.VMEM((3, rows, width), BF),
            pltpu.VMEM((rows, width), F32),
            pltpu.VMEM((4, 512, 512), BF),
            sems((4,)),
            sems((4 + 4 * length,)),
            sems((8,)),
            sems((8,)),
            sems((7,)),
            sems((7,)),
        ],
        compiler_params=pltpu.CompilerParams(
            collective_id=1, has_side_effects=True, vmem_limit_bytes=60 << 20
        ),
        cost_estimate=pl.CostEstimate(
            flops=12 * 8 * rows * width * hidden, bytes_accessed=40 << 20, transcendentals=0
        ),
    )(second, down_all, up_mine, ubias, down_mine)


ROW_TILE = 32


def for_rows(total, fn):
    @pl.loop(0, total // ROW_TILE)
    def step(index):
        fn(pl.ds(pl.multiple_of(index * ROW_TILE, ROW_TILE), ROW_TILE))


def norm_rows(values):
    center = values - jnp.mean(values, axis=-1, keepdims=True)
    spread = jnp.mean(center * center, axis=-1, keepdims=True)
    rstd = lax.rsqrt(spread + EPSILON)
    return center * rstd, rstd


class Gathered:
    def __init__(self, shard_ref, full_ref, sems, base, where):
        self.y, self.c, self.x = where
        self.shard, self.full, self.sems, self.base = shard_ref, full_ref, sems, base
        self.rows = shard_ref.shape[0]
        self.half = self.rows // 2
        self.step = self.half // 4
        self.place = self.y * 2 + self.c

    def copy(self, src, dst, index, device):
        send_sems, recv_sems = self.sems
        return remote(src, dst, send_sems, recv_sems, self.base + index, device)

    def span(self, place, side, i):
        start = place * self.rows + side * self.half + i * self.step
        return self.full.at[pl.ds(pl.multiple_of(start, self.step), self.step)]

    def over_y(self, i):
        start = pl.multiple_of(self.x * self.half + i * self.step, self.step)
        return self.copy(
            self.shard.at[pl.ds(start, self.step)], self.span(self.place, self.x, i), i, {"y": 1 - self.y}
        )

    def over_x(self, i):
        ref = self.span(self.place ^ 2, self.x, i)
        return self.copy(ref, ref, 4 + i, {"x": 1 - self.x})

    def over_c(self, i, side):
        ref = self.span(self.place ^ 2, self.x if side == 0 else 1 - self.x, i)
        return self.copy(ref, ref, 8 + 4 * side + i, {"c": 1 - self.c})

    def own_c(self):
        start = pl.multiple_of(self.place * self.rows, self.rows)
        return self.copy(self.shard, self.full.at[pl.ds(start, self.rows)], 16, {"c": 1 - self.c})

    def settle(self):
        self.own_c().wait_recv()
        for i in range(4):
            self.over_c(i, 0).wait_recv()
            self.over_c(i, 1).wait_recv()

    def own(self, sem):
        start = pl.multiple_of(self.place * self.rows, self.rows)
        return pltpu.make_async_copy(self.shard, self.full.at[pl.ds(start, self.rows)], sem)


class WeightStep:
    def __init__(self, weight, i):
        self.weight, self.i = weight, i

    def start(self, begin):
        begin(self.weight.over_y(self.i))

    def arrive(self):
        self.weight.over_y(self.i).wait_recv()

    def follow(self, begin):
        begin(self.weight.over_x(self.i))
        begin(self.weight.over_c(self.i, 0))

    def late(self, begin):
        self.weight.over_x(self.i).wait_recv()
        begin(self.weight.over_c(self.i, 1))


class Stream:
    def __init__(self, order, begin):
        self.order, self.begin = order, begin
        self.next = 0
        self.behind = None
        for step in order[:2]:
            step.start(begin)

    def event(self):
        n = self.next
        self.next += 1
        step = self.order[n]
        step.arrive()
        if n + 2 < len(self.order):
            self.order[n + 2].start(self.begin)
        step.follow(self.begin)
        self.late()
        self.behind = step

    def late(self):
        if self.behind is not None:
            self.behind.late(self.begin)
        self.behind = None


def front_kernel(
    lengths_ref,
    tokens_v,
    smalls_ref,
    kvw_ref,
    qw_ref,
    mw_ref,
    up_ref,
    cot_ref,
    second_ref,
    residual_ref,
    first_v,
    q_v,
    kv_v,
    mixed_v,
    lse_ref,
    vec_v,
    wq_out,
    wm_out,
    wkv_v,
    up_out,
    cots_out,
    wq_v,
    wm_v,
    smalls_v,
    local_sem,
    w_send,
    w_recv,
    s_send,
    s_recv,
    k_send,
    k_recv,
    u_send,
    u_recv,
    uz_send,
    uz_recv,
    c_send,
    c_recv,
    *,
    length,
    slots,
    with_length,
    aligned,
):
    rows, width = tokens_v.shape
    seg = rows // slots
    head_dim = kvw_ref.shape[1] // 2
    heads = width // head_dim
    group = 4
    quarter = width // 4
    y, c, z, x = [lax.axis_index(name) for name in ("y", "c", "z", "x")]
    place = y * 2 + c
    sib, to_x, to_y = {"c": 1 - c}, {"x": 1 - x}, {"y": 1 - y}
    cross, diag = {"y": 1 - y, "c": 1 - c}, {"x": 1 - x, "y": 1 - y}

    weights = [
        Gathered(ref, full, (w_send, w_recv), 17 * n, (y, c, x))
        for n, (ref, full) in enumerate(((qw_ref, wq_v), (mw_ref, wm_v)))
    ]
    query_w, mixer_w = weights
    locals_ = [query_w.own(local_sem.at[0]), mixer_w.own(local_sem.at[1])]
    kv_rows = pl.ds(pl.multiple_of(place * quarter, quarter), quarter)
    locals_.append(pltpu.make_async_copy(kvw_ref, wkv_v.at[kv_rows], local_sem.at[2]))
    locals_.append(pltpu.make_async_copy(smalls_ref, smalls_v.at[place], local_sem.at[3]))
    for copy in locals_:
        copy.start()

    barrier = pltpu.get_barrier_semaphore()
    for device in (sib, to_x, to_y, cross, diag):
        pl.semaphore_signal(barrier, inc=1, device_id=device, device_id_type=MESH)
    for other in range(length):
        @pl.when(other != z)
        def hello():
            pl.semaphore_signal(barrier, inc=1, device_id={"z": other}, device_id_type=MESH)
    pl.semaphore_wait(barrier, 5 + length - 1)

    sent = []

    def begin(copy):
        copy.start()
        sent.append(copy)
        return copy

    small_copies = [
        begin(remote(smalls_ref, smalls_v.at[place], s_send, s_recv, n, device))
        for n, device in enumerate((sib, to_y, cross))
    ]
    kv_near = begin(remote(kvw_ref, wkv_v.at[kv_rows], s_send, s_recv, 3, sib))
    kv_far = begin(remote(kvw_ref, wkv_v.at[kv_rows], s_send, s_recv, 4, to_y))
    part = quarter // length
    hidden = up_out.shape[1]
    block = hidden // length

    def up_copies(index, flip, span, device):
        target = place ^ flip
        dst_rows = pl.ds(pl.multiple_of(place * quarter + span[0], span[1]), span[1])
        copies = []
        for b in range(length if aligned else 1):
            if aligned:
                start = target * (hidden * 2) + (2 * b + x) * block
                src = up_ref.at[pl.ds(span[0], span[1]), pl.ds(pl.multiple_of(start, block), block)]
                dst = up_out.at[dst_rows, pl.ds(b * block, block)]
            else:
                src = up_ref.at[target, pl.ds(span[0], span[1])]
                dst = up_out.at[dst_rows]
            n = index * length + b
            if device is None:
                copies.append(pltpu.make_async_copy(src, dst, u_send.at[n]))
            else:
                copies.append(remote(src, dst, u_send, u_recv, n, device))
        return copies

    up_local = [] if aligned else up_copies(0, 0, (0, quarter), None)
    up_near = up_copies(1, 1, (0, quarter), sib)
    z_part = (pl.multiple_of(z * part, part), part)
    up_far = up_copies(2, 2, z_part, to_y) + up_copies(3, 3, z_part, cross)

    def up_share(k, source, target):
        start = (place ^ (2 + k)) * quarter + source * part
        ref = up_out.at[pl.ds(pl.multiple_of(start, part), part)]
        return pltpu.make_async_remote_copy(
            src_ref=ref,
            dst_ref=ref,
            send_sem=uz_send.at[k, target],
            recv_sem=uz_recv.at[k, source],
            device_id={"z": target},
            device_id_type=MESH,
        )

    class UpStep:
        def start(self, begin):
            for copy in up_far:
                begin(copy)

        def arrive(self):
            for copy in up_far:
                copy.wait_recv()

        def follow(self, begin):
            for target in range(length):
                @pl.when(target != z)
                def share():
                    for k in range(2):
                        up_share(k, z, target).start()

        def late(self, begin):
            pass

    stream = Stream(
        [WeightStep(query_w, i) for i in range(4)] + [UpStep()] + [WeightStep(mixer_w, i) for i in range(4)],
        begin,
    )
    for weight in weights:
        begin(weight.own_c())

    for copy in small_copies:
        copy.wait_recv()
    locals_[3].wait()
    vec_v[...] = jnp.concatenate([smalls_v[f].astype(F32) for f in range(4)], axis=1)

    def first_norm(span):
        unit, _ = norm_rows(tokens_v[span, :].astype(F32))
        first_v[span, :] = (unit * vec_v[0:1, :] + vec_v[1:2, :]).astype(BF)

    for_rows(rows, first_norm)

    kv_far.wait_recv()
    far_rows = wkv_v.at[pl.ds(pl.multiple_of((place ^ 2) * quarter, quarter), quarter)]
    kv_pass = begin(remote(far_rows, far_rows, s_send, s_recv, 5, sib))
    stream.event()
    kv_near.wait_recv()
    locals_[2].wait()
    kv_pass.wait_recv()
    v_bias = (
        vec_v[7:8, 0:head_dim]
        + vec_v[7:8, quarter : quarter + head_dim]
        + vec_v[7:8, 2 * quarter : 2 * quarter + head_dim]
        + vec_v[7:8, 3 * quarter : 3 * quarter + head_dim]
    )
    keyvals = dot(first_v[...], wkv_v[...]) + jnp.concatenate([jnp.zeros_like(v_bias), v_bias], axis=1)
    mine = pl.ds(pl.multiple_of(x * seg, seg), seg)
    for s in range(slots):
        kv_v[s, 0, mine, :] = keyvals[s * seg : (s + 1) * seg].astype(BF)

    def kv_up(t):
        return remote(kv_v.at[:, t - 1, mine], kv_v.at[:, t, mine], k_send, k_recv, t, {"z": z + 1})

    def kv_side(t):
        ref = kv_v.at[:, t, mine]
        return remote(ref, ref, k_send, k_recv, length + t, to_x)

    def kv_step(t):
        if t:
            @pl.when(z >= t)
            def arrive():
                kv_up(t).wait_recv()

        @pl.when(z >= t)
        def side():
            kv_side(t).start()

        if t + 1 < length:
            @pl.when((z >= t) & (z < length - 1))
            def onward():
                kv_up(t + 1).start()

    for copy in up_local:
        copy.start()
    for copy in up_near:
        begin(copy)

    for t in range(length):
        kv_step(t)
        if t < 3:
            stream.event()

    same, other_half = pl.ds(0, rows), pl.ds(rows, rows)
    top, bottom = pl.ds(0, rows // 2), pl.ds(rows // 2, rows // 2)
    if not aligned:
        cot_local = pltpu.make_async_copy(cot_ref, cots_out.at[0, same], local_sem.at[4])
        cot_local.start()
    cot_x = remote(cot_ref, cots_out.at[1, same], c_send, c_recv, 0, to_x)
    cot_y = remote(cot_ref, cots_out.at[2, same], c_send, c_recv, 1, to_y)
    cot_share = [
        remote(cot_ref if k == 0 else cots_out.at[k, same], cots_out.at[k, other_half], c_send, c_recv, 2 + k, sib)
        for k in range(4)
    ]
    cot_dx = remote(cots_out.at[2, top], cots_out.at[3, top], c_send, c_recv, 6, to_x)
    cot_dy = remote(cots_out.at[1, bottom], cots_out.at[3, bottom], c_send, c_recv, 7, to_y)

    stream.late()
    locals_[0].wait()
    query_w.settle()

    @tiles(width // 512, 512)
    def project(cols, _):
        q_v[:, cols] = (dot(first_v[...], wq_v[:, cols]) + vec_v[2:3, cols]).astype(BF)

    wq_copy = pltpu.make_async_copy(wq_v, wq_out, local_sem.at[5])
    wq_copy.start()
    for t in range(length):
        @pl.when(z >= t)
        def arrived():
            kv_side(t).wait_recv()
            kv_side(t).wait_send()

        if t:
            @pl.when((z >= t - 1) & (z < length - 1))
            def gone():
                kv_up(t).wait_send()

    scale = head_dim ** (-0.5)

    def attend(s, g):
        lanes = pl.ds(pl.multiple_of(g * group * head_dim, group * head_dim), group * head_dim)
        wide = q_v[pl.ds(s * seg, seg), lanes]
        queries = jnp.concatenate(
            [wide[:, h * head_dim : (h + 1) * head_dim] for h in range(group)], axis=0
        )

        def step(t, state, diagonal):
            top_, total, accum = state
            keys = kv_v[s, t, :, :head_dim]
            values = kv_v[s, t, :, head_dim:]
            scores = dot(keys, queries, ((1,), (1,))) * scale
            if diagonal or with_length:
                key_pos = lax.broadcasted_iota(jnp.int32, (2 * seg, seg), 0)
                allowed = None
                if diagonal:
                    query_pos = lax.broadcasted_iota(jnp.int32, (2 * seg, seg), 1) + x * seg
                    allowed = key_pos <= query_pos
                if with_length:
                    inside = key_pos + (z - t) * (2 * seg) < lengths_ref[s]
                    allowed = inside if allowed is None else allowed & inside
                bias = jnp.where(allowed, 0.0, NEG_LARGE).astype(F32)
                scores = scores + jnp.concatenate([bias] * group, axis=1)
            new_top = jnp.maximum(top_, jnp.max(scores, axis=0, keepdims=True))
            terms = jnp.exp(scores - new_top)
            fade = jnp.exp(top_ - new_top)
            total = total * fade + jnp.sum(terms, axis=0, keepdims=True)
            accum = accum * fade + dot(values, terms.astype(BF), ((0,), (0,)))
            return new_top, total, accum

        span = group * seg
        state = (
            jnp.full((1, span), NEG_LARGE, F32),
            jnp.zeros((1, span), F32),
            jnp.zeros((head_dim, span), F32),
        )
        state = step(0, state, True)
        top_, total, accum = lax.fori_loop(1, z + 1, lambda t, st: step(t, st, False), state)
        out = accum / total
        mixed_v[pl.ds(s * seg, seg), lanes] = jnp.concatenate(
            [out[:, h * seg : (h + 1) * seg].T for h in range(group)], axis=1
        ).astype(BF)
        lse_ref[s, g] = top_ + jnp.log(total)

    for s in range(slots):
        for g in range(heads // group):
            attend(s, g)
            if stream.next < len(stream.order):
                stream.event()
                if stream.next == len(stream.order) - 1:
                    begin(cot_x)
                    begin(cot_y)
                    begin(cot_share[0])

    stream.late()
    locals_[1].wait()
    mixer_w.settle()
    wm_copy = pltpu.make_async_copy(wm_v, wm_out, local_sem.at[6])
    wm_copy.start()

    @tiles(width // 512, 512)
    def mix(cols, _):
        residual_ref[:, cols] = (
            tokens_v[:, cols].astype(F32) + dot(mixed_v[...], wm_v[:, cols]) + vec_v[3:4, cols]
        )

    def second_norm(span):
        unit, _ = norm_rows(residual_ref[span, :])
        second_ref[span, :] = (unit * vec_v[4:5, :] + vec_v[5:6, :]).astype(BF)

    for_rows(rows, second_norm)

    cot_x.wait_recv()
    cot_y.wait_recv()
    begin(cot_share[1])
    begin(cot_share[2])
    if not aligned:
        begin(cot_dx)
        begin(cot_dy)
        cot_dx.wait_recv()
        cot_dy.wait_recv()
        begin(cot_share[3])
    for copy in cot_share[: 3 if aligned else 4] + up_near:
        copy.wait_recv()
    for copy in up_local:
        copy.wait()
    for target in range(length):
        @pl.when(target != z)
        def shared():
            for k in range(2):
                up_share(k, z, target).wait_send()
                up_share(k, target, z).wait_recv()
    for copy in sent:
        copy.wait_send()
    for copy in (wq_copy, wm_copy) + (() if aligned else (cot_local,)):
        copy.wait()


def front(lengths, tokens, smalls, kvw, qw, mw, up, cot, slots, length, with_length, aligned, hidden):
    rows, width = tokens.shape
    seg = rows // slots
    both = kvw.shape[1]
    groups = width // (both // 2) // 4
    hbm = pl.BlockSpec(memory_space=pltpu.HBM)
    vmem = pl.BlockSpec(memory_space=pltpu.VMEM)
    sems = pltpu.SemaphoreType.DMA
    return pl.pallas_call(
        functools.partial(
            front_kernel, length=length, slots=slots, with_length=with_length, aligned=aligned
        ),
        in_specs=[pl.BlockSpec(memory_space=pltpu.SMEM), vmem, hbm, hbm, hbm, hbm, hbm, hbm],
        out_specs=[vmem] * 8 + [hbm, hbm, vmem, hbm, hbm],
        out_shape=[
            jax.ShapeDtypeStruct((rows, width), BF),
            jax.ShapeDtypeStruct((rows, width), F32),
            jax.ShapeDtypeStruct((rows, width), BF),
            jax.ShapeDtypeStruct((rows, width), BF),
            jax.ShapeDtypeStruct((slots, length, 2 * seg, both), BF),
            jax.ShapeDtypeStruct((rows, width), BF),
            jax.ShapeDtypeStruct((slots, groups, 1, 4 * seg), F32),
            jax.ShapeDtypeStruct((16, width), F32),
            jax.ShapeDtypeStruct((width, width), BF),
            jax.ShapeDtypeStruct((width, width), BF),
            jax.ShapeDtypeStruct((width, both), BF),
            jax.ShapeDtypeStruct((width, hidden), BF),
            jax.ShapeDtypeStruct((4, 2 * rows, width), BF),
        ],
        scratch_shapes=[
            pltpu.VMEM((width, width), BF),
            pltpu.VMEM((width, width), BF),
            pltpu.VMEM((4, 16, width // 4), BF),
            sems((7,)),
            sems((34,)),
            sems((34,)),
            sems((6,)),
            sems((6,)),
            sems((2 * length,)),
            sems((2 * length,)),
            sems((4 * length,)),
            sems((4 * length,)),
            sems((2, length)),
            sems((2, length)),
            sems((8,)),
            sems((8,)),
        ],
        compiler_params=pltpu.CompilerParams(
            collective_id=2, has_side_effects=True, vmem_limit_bytes=60 << 20
        ),
        cost_estimate=pl.CostEstimate(
            flops=6 * rows * width * width, bytes_accessed=40 << 20, transcendentals=0
        ),
    )(lengths, tokens, smalls, kvw, qw, mw, up, cot)


def feed_kernel(
    second_ref,
    cot_ref,
    down_all_ref,
    up_ref,
    upw_ref,
    ubias_ref,
    residual_ref,
    vec_ref,
    down_ref,
    dres_ref,
    red_ref,
    down_part_ref,
    up_part_ref,
    ubias_part_ref,
    vsum_ref,
    tokens_v,
    cots_v,
    up_v,
    down_v,
    active_v,
    dupper_v,
    sib_out,
    sib_in,
    red_in,
    chip_out,
    chip_in,
    acc_v,
    stage_v,
    load_sem,
    stage_sem,
    gs_send,
    gs_recv,
    rs_send,
    rs_recv,
    *,
    length,
):
    rows, width = second_ref.shape
    hidden = up_ref.shape[1]
    half = rows // 2
    chunk = 2 * rows
    y, c, x = [lax.axis_index(name) for name in ("y", "c", "x")]
    sib, to_x, to_y = {"c": 1 - c}, {"x": 1 - x}, {"y": 1 - y}
    diag = {"x": 1 - x, "y": 1 - y}
    chips = (None, to_x, to_y, diag)

    loads = [
        pltpu.make_async_copy(second_ref, tokens_v.at[0, pl.ds(0, rows)], load_sem.at[0]),
        pltpu.make_async_copy(cot_ref, cots_v.at[pl.ds(0, rows)], load_sem.at[1]),
        pltpu.make_async_copy(
            down_all_ref.at[pl.ds(rows, 5 * rows)], cots_v.at[pl.ds(rows, 5 * rows)], load_sem.at[2]
        ),
    ]
    block = hidden // length
    quarter = width // 4
    place = y * 2 + c
    ups_in = []
    for flip in range(1, 4):
        span = pl.ds(pl.multiple_of((place ^ flip) * quarter, quarter), quarter)
        ups_in.append(pltpu.make_async_copy(up_ref.at[span], up_v.at[span], load_sem.at[3 + flip]))
    own_rows = pl.ds(pl.multiple_of(place * quarter, quarter), quarter)
    for b in range(length):
        start = place * (2 * hidden) + (2 * b + x) * block
        ups_in.append(
            pltpu.make_async_copy(
                upw_ref.at[:, pl.ds(pl.multiple_of(start, block), block)],
                up_v.at[own_rows, pl.ds(b * block, block)],
                load_sem.at[7 + length + b],
            )
        )
    downs_in = [
        pltpu.make_async_copy(
            down_ref.at[pl.ds(pl.multiple_of((2 * b + x) * block, block), block)],
            down_v.at[pl.ds(b * block, block)],
            load_sem.at[7 + b],
        )
        for b in range(length)
    ]
    for load in loads + downs_in + ups_in:
        load.start()
    greet((sib, to_x, to_y, diag))
    loads[0].wait()

    same, other = pl.ds(0, rows), pl.ds(rows, rows)
    top, bottom = pl.ds(0, half), pl.ds(half, half)

    def gather(index, chip, span_src, chip_dst, span_dst, device):
        return remote(
            tokens_v.at[chip, span_src], tokens_v.at[chip_dst, span_dst], gs_send, gs_recv, index, device
        )

    send_x = gather(0, 0, same, 1, same, to_x)
    send_y = gather(1, 0, same, 2, same, to_y)
    share = [gather(2 + k, k, same, k, other, sib) for k in range(4)]
    diag_x = gather(6, 2, top, 3, top, to_x)
    diag_y = gather(7, 1, bottom, 3, bottom, to_y)
    send_x.start()
    send_y.start()
    share[0].start()

    loads[1].wait()
    loads[2].wait()
    for load in downs_in:
        load.wait()

    def cot_part(chip, start, size):
        return cots_v.at[pl.ds(chip * chunk + start, size)]

    cot_dx = remote(cot_part(2, 0, half), cot_part(3, 0, half), gs_send, gs_recv, 8, to_x)
    cot_dy = remote(cot_part(1, half, half), cot_part(3, half, half), gs_send, gs_recv, 9, to_y)
    cot_dc = remote(cot_part(3, 0, rows), cot_part(3, rows, rows), gs_send, gs_recv, 10, sib)
    cot_dx.start()
    cot_dy.start()

    def grad_active(span, index):
        @tiles(hidden // 512, 512)
        def columns(cols, _):
            dupper_v[span, cols] = dot(cots_v[span, :], down_v[cols, :], ((1,), (1,))).astype(BF)

    @pl.loop(0, 3)
    def near_grads(k):
        grad_active(pl.ds(pl.multiple_of(k * chunk, chunk), chunk), k)

    for load in ups_in:
        load.wait()

    def chip_work(k):
        @tiles(hidden // 256, 256)
        def columns(cols, _):
            block = pl.ds(k * chunk, chunk)
            upper = dot(tokens_v[k], up_v[:, cols]) + ubias_ref[:, cols]
            active, slope = gelu_pair(upper)
            active_v[block, cols] = active.astype(BF)
            d_upper = (dupper_v[block, cols].astype(F32) * slope).astype(BF)
            dupper_v[block, cols] = d_upper
            part = jnp.sum(d_upper.astype(F32), axis=0, keepdims=True)
            if k == 0:
                ubias_part_ref[:, cols] = part
            else:
                ubias_part_ref[:, cols] += part

        @tiles(width // 512, 512)
        def to_sibling(cols, _):
            sib_out[k, :, cols] = dot(
                dupper_v[pl.ds(k * chunk + rows, rows), :], up_v[cols, :], ((1,), (1,))
            ).astype(BF)

        pair = remote(sib_out.at[k], sib_in.at[k], rs_send, rs_recv, k, sib)
        pair.start()

        @tiles(width // 512, 512)
        def keep(cols, _):
            dres_ref[:, cols] = dot(dupper_v[pl.ds(k * chunk, rows), :], up_v[cols, :], ((1,), (1,)))

        pair.wait_recv()

        def total(span):
            value = dres_ref[span, :] + sib_in[k, span, :].astype(F32)
            if k == 0:
                acc_v[span, :] = value
            else:
                chip_out[k - 1, span, :] = value.astype(BF)

        for_rows(rows, total)
        if k == 0:
            return [pair]
        far = remote(chip_out.at[k - 1], chip_in.at[k - 1], rs_send, rs_recv, 3 + k, chips[k])
        far.start()
        return [pair, far]

    share[0].wait_recv()
    sent = chip_work(0)
    send_x.wait_recv()
    share[1].start()
    diag_y.start()
    send_y.wait_recv()
    share[2].start()
    diag_x.start()
    share[1].wait_recv()
    sent += chip_work(1)
    share[2].wait_recv()
    sent += chip_work(2)
    diag_x.wait_recv()
    diag_y.wait_recv()
    share[3].start()
    cot_dx.wait_recv()
    cot_dy.wait_recv()
    cot_dc.start()
    cot_dc.wait_recv()
    grad_active(pl.ds(3 * chunk, chunk), 3)
    share[3].wait_recv()
    sent += chip_work(3)

    def staged(slot, value, target):
        stage_v[slot] = value.astype(BF)
        copy = pltpu.make_async_copy(stage_v.at[slot], target, stage_sem.at[slot])
        copy.start()
        return copy

    pairs = []
    for k in range(4):
        sent[0 if k == 0 else 2 * k - 1].wait_send()

        @tiles(width // 512, 512)
        def to_sibling(cols, _):
            sib_out[k, :, cols] = dot(
                active_v[pl.ds(k * chunk + rows, rows), :], down_v[:, cols]
            ).astype(BF)

        pair = remote(sib_out.at[k], red_in.at[k], rs_send, rs_recv, 7 + k, sib)
        pair.start()
        pairs.append(pair)

    for k in range(4):

        @tiles(width // 512, 512)
        def keep(cols, _):
            dres_ref[:, cols] = dot(active_v[pl.ds(k * chunk, rows), :], down_v[:, cols])

        pairs[k].wait_recv()

        def total(span):
            red_in[k, span, :] = (dres_ref[span, :] + red_in[k, span, :].astype(F32)).astype(BF)

        for_rows(rows, total)
    red_copy = pltpu.make_async_copy(red_in, red_ref, load_sem.at[3])
    red_copy.start()

    @pl.loop(0, hidden // 512)
    def downs(r):
        block = pl.ds(pl.multiple_of(r * 512, 512), 512)
        copies = []
        for j in range(width // 512):
            cols = pl.ds(j * 512, 512)
            copies.append(
                staged(
                    j,
                    dot(active_v[:, block], cots_v[:, cols], ((0,), (0,))),
                    down_part_ref.at[block, cols],
                )
            )
        for copy in copies:
            copy.wait()

    piece = quarter // length

    @pl.loop(0, hidden // 512)
    def ups(r):
        first = pl.multiple_of(r * 512, 512)
        cols = pl.ds(first, 512)
        copies = []
        for f in range(4):
            value = None
            for k in range(4):
                term = dot(
                    tokens_v[k, :, f * quarter : (f + 1) * quarter],
                    dupper_v[k * chunk : (k + 1) * chunk, cols],
                    ((0,), (0,)),
                )
                value = term if value is None else value + term
            stage_v[f] = value.astype(BF)
            for level in range(length):
                copy = pltpu.make_async_copy(
                    stage_v.at[f, pl.ds(level * piece, piece)],
                    up_part_ref.at[
                        level, pl.ds((f % 2) * piece, piece), pl.ds((f // 2) * hidden + first, 512)
                    ],
                    stage_sem.at[4 + f * length + level],
                )
                copy.start()
                copies.append(copy)
        for copy in copies:
            copy.wait()

    for k in range(3):
        remote(chip_out.at[k], chip_in.at[k], rs_send, rs_recv, 4 + k, chips[k + 1]).wait_recv()
    vsum_ref[...] = jnp.zeros(vsum_ref.shape, F32)

    def norm_back(span):
        d_second = acc_v[span, :]
        for k in range(3):
            d_second = d_second + chip_in[k, span, :].astype(F32)
        unit, rstd = norm_rows(residual_ref[span, :])
        d_out = cots_v[span, :].astype(F32)
        d_residual = d_out + norm_backward(d_second, unit, rstd, vec_ref[4:5, :])
        dres_ref[span, :] = d_residual
        vsum_ref[0:1, :] += jnp.sum(d_second * unit, axis=0, keepdims=True)
        vsum_ref[1:2, :] += jnp.sum(d_second, axis=0, keepdims=True)
        vsum_ref[2:3, :] += jnp.sum(d_residual.astype(BF).astype(F32), axis=0, keepdims=True)
        vsum_ref[3:4, :] += jnp.sum(d_out, axis=0, keepdims=True)

    for_rows(rows, norm_back)
    red_copy.wait()
    for copy in [send_x, send_y, diag_x, diag_y, cot_dx, cot_dy, cot_dc] + share + pairs + sent[2::2]:
        copy.wait_send()


def feed(second, d_down, down_all, up_mine, up_weight, ubias, residual, vectors, down_weight, length):
    rows, width = second.shape
    hidden = up_mine.shape[1]
    hbm = pl.BlockSpec(memory_space=pltpu.HBM)
    vmem = pl.BlockSpec(memory_space=pltpu.VMEM)
    sems = pltpu.SemaphoreType.DMA
    return pl.pallas_call(
        functools.partial(feed_kernel, length=length),
        in_specs=[hbm, hbm, hbm, hbm, hbm, vmem, vmem, vmem, hbm],
        out_specs=[vmem, hbm, hbm, hbm, vmem, vmem],
        out_shape=[
            jax.ShapeDtypeStruct((rows, width), F32),
            jax.ShapeDtypeStruct((4, rows, width), BF),
            jax.ShapeDtypeStruct((hidden, width), BF),
            jax.ShapeDtypeStruct((length, hidden // length, width), BF),
            jax.ShapeDtypeStruct((1, hidden), F32),
            jax.ShapeDtypeStruct((8, width), F32),
        ],
        scratch_shapes=[
            pltpu.VMEM((4, 2 * rows, width), BF),
            pltpu.VMEM((8 * rows, width), BF),
            pltpu.VMEM((width, hidden), BF),
            pltpu.VMEM((hidden, width), BF),
            pltpu.VMEM((8 * rows, hidden), BF),
            pltpu.VMEM((8 * rows, hidden), BF),
            pltpu.VMEM((4, rows, width), BF),
            pltpu.VMEM((4, rows, width), BF),
            pltpu.VMEM((4, rows, width), BF),
            pltpu.VMEM((3, rows, width), BF),
            pltpu.VMEM((3, rows, width), BF),
            pltpu.VMEM((rows, width), F32),
            pltpu.VMEM((4, 512, 512), BF),
            sems((7 + 2 * length,)),
            sems((4 + 4 * length,)),
            sems((11,)),
            sems((11,)),
            sems((11,)),
            sems((11,)),
        ],
        compiler_params=pltpu.CompilerParams(
            collective_id=4, has_side_effects=True, vmem_limit_bytes=62 << 20
        ),
        cost_estimate=pl.CostEstimate(
            flops=12 * 8 * rows * width * hidden, bytes_accessed=40 << 20, transcendentals=0
        ),
    )(second, d_down, down_all, up_mine, up_weight, ubias, residual, vectors, down_weight)


class Links:
    def __init__(self, send_sems, recv_sems, count):
        self.send_sems, self.recv_sems, self.count = send_sems, recv_sems, count
        self.used = 0

    def copy(self, src, dst, device):
        index = self.used
        self.used += 1
        assert index < self.count
        return self.again(src, dst, device, index)

    def again(self, src, dst, device, index):
        return remote(src, dst, self.send_sems, self.recv_sems, index, device)


class LineSum:
    def __init__(self, links, z, length, parts, landing):
        self.z, self.length, self.parts, self.landing = z, length, parts, landing
        self.copies = {}
        self.links = links

    def position(self, way):
        return self.z if way == 0 else self.length - 1 - self.z

    def block(self, way, t):
        index = self.length - t + self.position(way)
        index = index if way == 0 else self.length - 1 - index
        return jnp.clip(index, 0, self.length - 1)

    def clear(self):
        last = self.length - 1
        for way in range(2):
            @pl.when(self.position(way) == 0)
            def zero():
                ref = self.landing(way, last)
                ref[...] = jnp.zeros(ref.shape, ref.dtype)

    def step(self, t):
        if t > 1:
            self.settle(t - 1)
        for way in range(2):
            pos = self.position(way)
            device = {"z": self.z + (1 if way == 0 else -1)}
            part = self.parts.at[self.block(way, t)]
            index = self.links.used
            direct = self.links.copy(part, self.landing(way, t), device)
            self.copies[way, t] = direct

            @pl.when(pos == 0)
            def first():
                direct.start()

            if t > 1:
                ref = self.landing(way, t - 1)
                passed = self.links.again(ref, self.landing(way, t), device, index)

                @pl.when((pos >= 1) & (pos <= t - 1))
                def onward():
                    self.copies[way, t - 1].wait_recv()
                    add_rows(ref, part)
                    passed.start()

    def finish(self, own, out):
        last = self.length - 1
        for way in range(2):
            @pl.when(self.position(way) >= 1)
            def arrive():
                self.copies[way, last].wait_recv()

        right, left = self.landing(0, last), self.landing(1, last)
        rows = out.shape[0]
        tile = min(rows, ROW_TILE)

        @pl.loop(0, rows // tile)
        def add(index):
            span = pl.ds(pl.multiple_of(index * tile, tile), tile)
            out[span, :] = (
                own[span, :].astype(F32) + right[span, :].astype(F32) + left[span, :].astype(F32)
            ).astype(out.dtype)

    def settle(self, t):
        for way in range(2):
            @pl.when((self.position(way) <= t - 1) & (self.position(way) < self.length - 1))
            def sent():
                self.copies[way, t].wait_send()

    def drain(self):
        self.settle(self.length - 1)


def add_rows(ref, term):
    rows = ref.shape[0]
    tile = min(rows, ROW_TILE)

    @pl.loop(0, rows // tile)
    def add(index):
        span = pl.ds(pl.multiple_of(index * tile, tile), tile)
        ref[span, :] = (ref[span, :].astype(F32) + term[span, :].astype(F32)).astype(ref.dtype)


class GradSum:
    def __init__(self, links, where, length, width, cols, left, right, bufs):
        self.y, self.c, self.z, self.x = where
        self.length, self.width, self.half = length, width, cols // 2
        self.left, self.right = left, right
        self.cols = cols
        (
            self.left_own,
            self.left_out,
            self.left_in,
            self.right_in,
            self.send1,
            self.recv1,
            self.send2,
            self.recv2,
            self.hold,
            self.zpart,
            self.zland,
        ) = bufs
        self.links = links
        self.sent = []

    def begin(self, copy):
        copy.start()
        self.sent.append(copy)
        return copy

    def all_cols(self, ref):
        return ref.at[..., pl.ds(0, self.cols)] if ref.shape[-1] != self.cols else ref

    def half_cols(self, ref):
        return ref.at[..., pl.ds(0, self.half)] if ref.shape[-1] != self.half else ref

    def share(self):
        quarter = self.width // 4
        block = quarter // (2 * self.length)
        for core, target in ((1 - self.c, self.left_out), (self.c, self.left_own)):
            for y_part in range(2):
                lanes = pl.ds(pl.multiple_of((y_part * 2 + core) * quarter, quarter), quarter)
                turned = self.left[:, lanes].astype(F32).T.astype(BF)
                for x_part in range(2):
                    for level in range(self.length):
                        start = (level * 2 + x_part) * block
                        target[y_part * 2 + x_part, level * block : (level + 1) * block, :] = turned[
                            start : start + block
                        ]
        sib = {"c": 1 - self.c}
        self.left_copy = self.begin(self.links.copy(self.left_out, self.left_in, sib))
        self.right_copy = self.begin(self.links.copy(self.right, self.all_cols(self.right_in), sib))

    def term(self, y_part, x_part, cols):
        g = y_part * 2 + x_part
        return dot(self.left_own[g], self.right[:, cols]) + dot(self.left_in[g], self.right_in[:, cols])

    def columns(self, side, fn):
        count = self.half // 128
        size = 128 * max(n for n in range(1, 5) if count % n == 0)
        for j in range(self.half // size):
            fn(pl.ds(side * self.half + j * size, size), pl.ds(j * size, size))

    def first(self):
        self.left_copy.wait_recv()
        self.right_copy.wait_recv()
        for n in range(2):

            def over_y(cols, local):
                self.send1[0, n, :, local] = self.term(1 - self.y, n, cols).astype(BF)

            def over_x(cols, local):
                self.send1[1, n, :, local] = self.term(n, 1 - self.x, cols).astype(BF)

            self.columns(0, over_y)
            self.columns(1, over_x)
        self.copies1 = [
            self.begin(
                self.links.copy(self.half_cols(self.send1.at[side]), self.half_cols(self.recv1.at[side]), device)
            )
            for side, device in ((0, {"y": 1 - self.y}), (1, {"x": 1 - self.x}))
        ]

    def second(self):
        for copy in self.copies1:
            copy.wait_recv()

        def a_out(cols, local):
            term = self.term(self.y, 1 - self.x, cols) + self.recv1[0, 1 - self.x, :, local].astype(F32)
            self.send2[0, :, local] = term.astype(BF)

        def b_out(cols, local):
            term = self.term(1 - self.y, self.x, cols) + self.recv1[1, 1 - self.y, :, local].astype(F32)
            self.send2[1, :, local] = term.astype(BF)

        def a_keep(cols, local):
            self.hold[:, cols] = self.term(self.y, self.x, cols) + self.recv1[0, self.x, :, local].astype(F32)

        def b_keep(cols, local):
            self.hold[:, cols] = self.term(self.y, self.x, cols) + self.recv1[1, self.y, :, local].astype(F32)

        self.columns(0, a_out)
        self.columns(1, b_out)
        self.copies2 = [
            self.begin(
                self.links.copy(self.half_cols(self.send2.at[side]), self.half_cols(self.recv2.at[side]), device)
            )
            for side, device in ((0, {"x": 1 - self.x}), (1, {"y": 1 - self.y}))
        ]
        self.columns(0, a_keep)
        self.columns(1, b_keep)

    def third(self, out):
        for copy in self.copies2:
            copy.wait_recv()
        block = self.hold.shape[0] // self.length
        for side in range(2):

            def add(cols, local):
                total = self.hold[:, cols] + self.recv2[side, :, local].astype(F32)
                self.hold[:, cols] = total
                for level in range(self.length):
                    self.zpart[level, :, cols] = total[level * block : (level + 1) * block].astype(BF)

            self.columns(side, add)
        rows = pl.ds(pl.multiple_of(self.z * block, block), block)
        out[...] = self.all_cols(self.hold)[rows, :]
        self.line = LineSum(
            self.links,
            self.z,
            self.length,
            self.all_cols(self.zpart),
            lambda way, t: self.all_cols(self.zland.at[way, t - 1]),
        )

    def finish(self, out):
        self.line.finish(out, out)

    def drain(self):
        for copy in self.sent:
            copy.wait_send()
        self.line.drain()


def back_kernel(
    lengths_ref,
    tokens_v,
    dres_ref,
    first_ref,
    q_ref,
    kv_ref,
    mixed_ref,
    lse_ref,
    vec_ref,
    wkv_ref,
    vsum_ref,
    ubias_ref,
    wq_ref,
    wm_ref,
    red_ref,
    down_part,
    up_part,
    tgrad_ref,
    query_ref,
    mixer_ref,
    up_ref,
    vectors_ref,
    far_ref,
    down_last,
    w_v,
    dmix_v,
    dmixed_v,
    right_v,
    dfirst_v,
    dkv_v,
    keep_v,
    xsend_v,
    xrecv_v,
    csend_v,
    crecv_v,
    line_v,
    land_v,
    last_v,
    upsend_v,
    uprecv_v,
    vsend_v,
    vrecv_v,
    left_own,
    left_out,
    left_in,
    right_in,
    send1,
    recv1,
    send2,
    recv2,
    hold,
    zpart,
    zland,
    load_sem,
    credit,
    send_sems,
    recv_sems,
    *,
    length,
    slots,
    with_length,
    count,
):
    rows, width = tokens_v.shape
    seg = rows // slots
    both = wkv_ref.shape[1]
    head_dim = both // 2
    heads = width // head_dim
    group = 4
    y, c, z, x = [lax.axis_index(name) for name in ("y", "c", "z", "x")]
    place = y * 2 + c
    sib, to_x, to_y, diag = {"c": 1 - c}, {"x": 1 - x}, {"y": 1 - y}, {"x": 1 - x, "y": 1 - y}
    links = Links(send_sems, recv_sems, count)
    scale = head_dim ** (-0.5)

    def load(src, dst, n):
        copy = pltpu.make_async_copy(src, dst, load_sem.at[n])
        copy.start()
        return copy

    load_up = load(up_part, line_v.at[0], 0)
    load_down = load(down_part, line_v.at[1], 1)
    strip = w_v.shape[1]

    class Strips:
        def __init__(self, ref):
            self.ref, self.loads = ref, {}

        def start(self, j):
            if (j + 1) * strip <= width:
                self.loads[j] = load(self.ref.at[pl.ds(j * strip, strip)], w_v.at[j % 2], 2 + j % 2)

        def over(self, fn):
            for j in range(width // strip):
                self.loads[j].wait()
                fn(pl.ds(j * strip, strip), w_v.at[j % 2])
                self.start(j + 2)

    mixer_strips, query_strips = Strips(wm_ref), Strips(wq_ref)
    mixer_strips.start(0)
    mixer_strips.start(1)

    def landing(n, final):
        return lambda way, t: land_v.at[n, way, t - 1] if t < length - 1 else final.at[way]

    up_line = LineSum(links, z, length, line_v.at[0], landing(0, last_v))
    down_line = LineSum(links, z, length, line_v.at[1], landing(1, down_last))
    bufs = (left_own, left_out, left_in, right_in, send1, recv1, send2, recv2, hold, zpart, zland)
    where = (y, c, z, x)
    mixer = GradSum(links, where, length, width, width, mixed_ref, dmix_v, bufs)
    query = GradSum(links, where, length, width, width + both, first_ref, right_v, bufs)
    up_line.clear()
    for way, edge in ((0, 0), (1, length - 1)):
        @pl.when(z == edge)
        def clear_edge():
            zland[way, length - 2] = jnp.zeros(zland.shape[2:], BF)

    @pl.when(z == length - 1)
    def clear_hops():
        crecv_v[...] = jnp.zeros(crecv_v.shape, BF)

    barrier = pltpu.get_barrier_semaphore()
    plane = []
    for flip in range(1, 8):
        device = {"y": y ^ (flip // 4), "c": c ^ (flip // 2 % 2), "x": x ^ (flip % 2)}
        plane.append(device)
    for device in plane:
        pl.semaphore_signal(barrier, inc=1, device_id=device, device_id_type=MESH)
    for other in range(length):
        @pl.when(other != z)
        def hello():
            pl.semaphore_signal(barrier, inc=1, device_id={"z": other}, device_id_type=MESH)
    pl.semaphore_wait(barrier, 7 + length - 1)

    sent = []

    def begin(copy):
        copy.start()
        sent.append(copy)
        return copy

    def hand_over(base):
        for way, step in ((0, 1), (1, -1)):
            @pl.when((z + step >= 0) & (z + step < length))
            def free():
                pl.semaphore_signal(
                    credit.at[base + way], inc=1, device_id={"z": z + step}, device_id_type=MESH
                )

        for way, step in ((0, 1), (1, -1)):
            @pl.when((z - step >= 0) & (z - step < length))
            def freed():
                pl.semaphore_wait(credit.at[base + way], 1)

    load_up.wait()
    up_line.step(1)
    far = [
        links.copy(red_ref.at[k + 1], far_ref.at[k], device)
        for k, device in enumerate((to_x, to_y, diag))
    ]
    begin(far[0])
    begin(far[1])

    def to_bf(span):
        dmix_v[span, :] = dres_ref[span, :].astype(BF)

    for_rows(rows, to_bf)

    def mix_back(cols, strip_v):
        dmixed_v[:, cols] = dot(dmix_v[...], strip_v[...], ((1,), (1,))).astype(BF)

    mixer_strips.over(mix_back)
    query_strips.start(0)
    query_strips.start(1)

    def attend(s, g):
        lanes = pl.ds(pl.multiple_of(g * group * head_dim, group * head_dim), group * head_dim)
        span = pl.ds(s * seg, seg)

        def stack(wide):
            return jnp.concatenate(
                [wide[:, h * head_dim : (h + 1) * head_dim] for h in range(group)], axis=0
            )

        queries = stack(q_ref[span, lanes])
        d_mixed = stack(dmixed_v[span, lanes])
        inner = mixed_ref[span, lanes].astype(F32) * dmixed_v[span, lanes].astype(F32)
        delta = jnp.concatenate(
            [
                jnp.sum(inner[:, h * head_dim : (h + 1) * head_dim].T, axis=0, keepdims=True)
                for h in range(group)
            ],
            axis=1,
        )
        lse = lse_ref[s, g]

        def step(t, accum, diagonal):
            keys = kv_ref[s, t, :, :head_dim]
            values = kv_ref[s, t, :, head_dim:]
            scores = dot(keys, queries, ((1,), (1,))) * scale
            if diagonal or with_length:
                key_pos = lax.broadcasted_iota(jnp.int32, (2 * seg, seg), 0)
                allowed = None
                if diagonal:
                    query_pos = lax.broadcasted_iota(jnp.int32, (2 * seg, seg), 1) + x * seg
                    allowed = key_pos <= query_pos
                if with_length:
                    inside = key_pos + (z - t) * (2 * seg) < lengths_ref[s]
                    allowed = inside if allowed is None else allowed & inside
                bias = jnp.where(allowed, 0.0, NEG_LARGE).astype(F32)
                scores = scores + jnp.concatenate([bias] * group, axis=1)
            probs = jnp.exp(scores - lse)
            d_probs = dot(values, d_mixed, ((1,), (1,)))
            d_scores = (probs * (d_probs - delta)).astype(BF)
            dkv_v[t, :, :head_dim] += dot(d_scores, queries) * scale
            dkv_v[t, :, head_dim:] += dot(probs.astype(BF), d_mixed)
            return accum + dot(keys, d_scores, ((0,), (0,)))

        accum = step(0, jnp.zeros((head_dim, group * seg), F32), True)
        accum = lax.fori_loop(1, z + 1, lambda t, a: step(t, a, False), accum)
        right_v[span, lanes] = (
            jnp.concatenate([accum[:, h * seg : (h + 1) * seg].T for h in range(group)], axis=1) * scale
        ).astype(BF)

    x_copies = []
    for s in range(slots):
        for t in range(length):
            dkv_v[t] = jnp.zeros(dkv_v.shape[1:], F32)

        @pl.loop(0, heads // group)
        def over_groups(g):
            attend(s, g)

        for t in range(length):
            keep_v[s, t] = dkv_v[t, pl.ds(pl.multiple_of(x * seg, seg), seg), :].astype(BF)
            xsend_v[s, t] = dkv_v[t, pl.ds(pl.multiple_of((1 - x) * seg, seg), seg), :].astype(BF)
        x_copies.append(begin(links.copy(xsend_v.at[s], xrecv_v.at[s], to_x)))
        if s == 0:
            load_down.wait()
            down_line.step(1)
            mixer.share()

    up_line.step(2)
    mixer.first()
    begin(far[2])

    for copy in x_copies:
        copy.wait_recv()
    hops = [links.copy(csend_v.at[t - 1], crecv_v.at[t - 1], {"z": z - 1}) for t in range(1, length)]
    for t in range(length - 1, -1, -1):
        @pl.when(t <= z)
        def hop():
            if t + 1 < length:
                @pl.when(z < length - 1)
                def arrive():
                    hops[t].wait_recv()

            total = keep_v[:, t].astype(F32) + xrecv_v[:, t].astype(F32)
            if t + 1 < length:
                total = total + crecv_v[t].astype(F32)
            if t:
                csend_v[t - 1] = total.astype(BF)
                hops[t - 1].start()
            else:
                for s in range(slots):
                    right_v[s * seg : (s + 1) * seg, width:] = total[s].astype(BF)

    def first_back(cols, strip_v):
        dfirst_v[:, cols] = dot(right_v[:, :width], strip_v[...], ((1,), (1,))) + dot(
            right_v[:, width:], wkv_ref[cols, :], ((1,), (1,))
        )

    query_strips.over(first_back)
    mixer.second()
    down_line.step(2)

    mixer.third(mixer_ref)
    mixer.line.step(1)
    neighbours = ((0, sib), (1, to_y), (2, to_x))
    for n, device in neighbours:
        pl.semaphore_signal(credit.at[n], inc=1, device_id=device, device_id_type=MESH)
    for n, _ in neighbours:
        pl.semaphore_wait(credit.at[n], 1)
    for copy in mixer.sent:
        copy.wait_send()
    query.share()
    query.first()

    vsend_v[0] = jnp.zeros(vsend_v.shape[1:], F32)

    def first_norm_back(span):
        unit, rstd = norm_rows(tokens_v[span, :].astype(F32))
        d_first = dfirst_v[span, :]
        tgrad_ref[span, :] = (
            dres_ref[span, :] + norm_backward(d_first, unit, rstd, vec_ref[0:1, :])
        ).astype(BF)
        vsend_v[0, 0:1, :] += jnp.sum(d_first * unit, axis=0, keepdims=True)
        vsend_v[0, 1:2, :] += jnp.sum(d_first, axis=0, keepdims=True)
        d_right = right_v[span, :].astype(F32)
        vsend_v[0, 2:3, :] += jnp.sum(d_right[:, :width], axis=0, keepdims=True)
        vsend_v[0, 3:4, 0:both] += jnp.sum(d_right[:, width:], axis=0, keepdims=True)

    for_rows(rows, first_norm_back)
    vsend_v[0, 4:8, :] = vsum_ref[0:4, :]
    vsend_v[0, 8:9, 0 : ubias_ref.shape[1]] = ubias_ref[...]

    partners = [(sib, 8), (to_x, 8), (to_y, 8)]
    bit = 1
    while bit < length:
        partners.append(({"z": z ^ bit}, 16))
        bit *= 2

    def exchange(n):
        device, high = partners[n]
        copy = begin(links.copy(vsend_v.at[n, pl.ds(0, high)], vrecv_v.at[n, pl.ds(0, high)], device))

        def land():
            copy.wait_recv()
            out = vectors_ref if n + 1 == len(partners) else vsend_v.at[n + 1]
            out[0:high, :] = vsend_v[n, 0:high, :] + vrecv_v[n, 0:high, :]
            if high == 8:
                out[8:16, :] = vsend_v[n, 8:16, :]

        return land

    land = exchange(0)
    up_line.step(3)
    land()
    land = exchange(1)
    mixer.line.step(2)
    land()
    land = exchange(2)
    query.second()
    land()
    land = exchange(3)
    down_line.step(3)
    for t in range(3, length):
        mixer.line.step(t)
    land()
    land = exchange(4)
    mixer.finish(mixer_ref)
    mixer.line.drain()
    hand_over(3)
    query.third(query_ref)
    query.line.step(1)
    land()

    upsum_v = dmixed_v
    up_line.finish(line_v.at[0, z], upsum_v)
    hidden = upsum_v.shape[1] // 2
    piece = upsum_v.shape[0] // 2
    block = piece // 2
    for f in range(4):
        for x_part in range(2):
            start = (f % 2) * piece + x_part * block
            lanes = slice((f // 2) * hidden, (f // 2 + 1) * hidden)
            upsend_v[f * 2 + x_part] = upsum_v[start : start + block, lanes]
    mine = place * 2 + x
    up_copies = []
    for flip, device in zip(range(1, 8), plane):
        up_copies.append(begin(links.copy(upsend_v.at[mine ^ flip], uprecv_v.at[flip], device)))
    out_block = hidden // length

    def place_up(flip, ref):
        source = mine ^ flip
        base = (source // 2) * (2 * hidden) + (source % 2) * out_block
        for level in range(length):
            lanes = pl.ds(pl.multiple_of(base + level * 2 * out_block, out_block), out_block)
            up_ref[:, lanes] = ref[:, level * out_block : (level + 1) * out_block].astype(up_ref.dtype)

    query.line.step(2)
    place_up(0, upsend_v.at[mine])
    for flip, copy in zip(range(1, 8), up_copies):
        copy.wait_recv()
        place_up(flip, uprecv_v.at[flip])
    for t in range(3, length):
        query.line.step(t)
    for copy in far:
        copy.wait_recv()
    query.finish(query_ref)
    for way in range(2):
        @pl.when(down_line.position(way) >= 1)
        def down_landed():
            down_line.copies[way, length - 1].wait_recv()
    for copy in sent:
        copy.wait_send()
    query.drain()
    up_line.drain()
    down_line.drain()
    for t in range(1, length):
        @pl.when(t <= z)
        def hopped():
            hops[t - 1].wait_send()


def back(lengths, vmem_args, hbm_args, slots, length, with_length):
    tokens, kv, wkv = vmem_args[0], vmem_args[4], vmem_args[8]
    rows, width = tokens.shape
    seg = rows // slots
    both = wkv.shape[1]
    cols = width + both
    hidden = width // 2
    block = width // (8 * length)
    stages = 3 + (length - 1).bit_length()
    count = 96 + 12 * length
    hbm = pl.BlockSpec(memory_space=pltpu.HBM)
    vmem = pl.BlockSpec(memory_space=pltpu.VMEM)
    sems = pltpu.SemaphoreType.DMA

    def half(*dims):
        return pltpu.VMEM(dims, BF)

    return pl.pallas_call(
        functools.partial(
            back_kernel, length=length, slots=slots, with_length=with_length, count=count
        ),
        in_specs=[pl.BlockSpec(memory_space=pltpu.SMEM)]
        + [vmem] * len(vmem_args)
        + [hbm] * len(hbm_args),
        out_specs=[vmem] * 5 + [hbm, hbm],
        out_shape=[
            jax.ShapeDtypeStruct((rows, width), BF),
            jax.ShapeDtypeStruct((block, cols), F32),
            jax.ShapeDtypeStruct((block, width), F32),
            jax.ShapeDtypeStruct((block, 8 * hidden), BF),
            jax.ShapeDtypeStruct((16, width), F32),
            jax.ShapeDtypeStruct((3, rows, width), BF),
            jax.ShapeDtypeStruct((2, hidden // length, width), BF),
        ],
        scratch_shapes=[
            half(2, width // 4, width),
            half(rows, width),
            half(rows, width),
            half(rows, cols),
            pltpu.VMEM((rows, width), F32),
            pltpu.VMEM((length, 2 * seg, both), F32),
            half(slots, length, seg, both),
            half(slots, length, seg, both),
            half(slots, length, seg, both),
            half(length - 1, slots, seg, both),
            half(length - 1, slots, seg, both),
            half(2, length, hidden // length, width),
            half(2, 2, length - 2, hidden // length, width),
            half(2, hidden // length, width),
            half(8, block, hidden),
            half(8, block, hidden),
            pltpu.VMEM((stages, 16, width), F32),
            pltpu.VMEM((stages, 16, width), F32),
            half(4, width // 8, rows),
            half(4, width // 8, rows),
            half(4, width // 8, rows),
            half(rows, cols),
            half(2, 2, width // 8, cols // 2),
            half(2, 2, width // 8, cols // 2),
            half(2, width // 8, cols // 2),
            half(2, width // 8, cols // 2),
            pltpu.VMEM((width // 8, cols), F32),
            half(length, block, cols),
            half(2, length - 1, block, cols),
            sems((4,)),
            pltpu.SemaphoreType.REGULAR((5,)),
            sems((count,)),
            sems((count,)),
        ],
        compiler_params=pltpu.CompilerParams(
            collective_id=3, has_side_effects=True, vmem_limit_bytes=62 << 20
        ),
        cost_estimate=pl.CostEstimate(
            flops=12 * rows * width * width, bytes_accessed=40 << 20, transcendentals=0
        ),
    )(lengths, *vmem_args, *hbm_args)


def finish_fast(given, kept, weights):
    tokens, lengths, d_down, up_weight, down_weight, up_bias, where, slots, length, with_length = given
    second, residual, first, queries, kv_all, mixed, lse, vectors = kept
    full_query, full_mixer, full_keyval, up_mine, down_all = weights
    y, c, z, x = where
    rows, width = second.shape
    flat = tokens.reshape(rows, width)
    d_residual, reduced, down_part, up_part, ubias_part, vsum = feed(
        second, d_down, down_all, up_mine, up_weight, up_bias, residual, vectors, down_weight, length
    )
    tokens_grad, query_all, mixer_grad, up_grad, sums, far, down_last = back(
        lengths,
        (flat, d_residual, first, queries, kv_all, mixed, lse, vectors, full_keyval, vsum, ubias_part),
        (full_query, full_mixer, reduced, down_part.reshape(length, -1, width), up_part),
        slots,
        length,
        with_length,
    )
    down_grad = pick(down_part.reshape(length, -1, width), z, 0).astype(F32)
    down_grad = down_grad + jnp.where(z > 0, down_last[0].astype(F32), 0.0)
    down_grad = down_grad + jnp.where(z < length - 1, down_last[1].astype(F32), 0.0)
    output = residual + vectors[6:7]
    for term in (reduced[0], far[0], far[1], far[2]):
        output = output + term.astype(F32)
    layer_out = output.astype(BF).reshape(tokens.shape)
    devices = 8 * length
    index = (y * 2 + c) * 2 * length + z * 2 + x
    block = width // devices
    mine = lax.dynamic_slice_in_dim(sums[:8], index * block, block, 1)
    head_dim = full_keyval.shape[1] // 2
    v_block = head_dim // devices
    vbias = lax.dynamic_slice_in_dim(sums[3], head_dim + index * v_block, v_block, 0)
    u_block = up_bias.shape[1] // length
    ubias = lax.dynamic_slice_in_dim(sums[8], z * u_block, u_block, 0)
    return (
        layer_out,
        tokens_grad.reshape(tokens.shape),
        mine[0],
        mine[1],
        query_all[:, :width],
        mine[2],
        query_all[:, width:],
        vbias,
        mixer_grad,
        mine[6],
        mine[4],
        mine[5],
        up_grad.astype(F32),
        ubias,
        down_grad,
        mine[7],
    )


def body(
    tokens,
    lengths,
    cotangent,
    norm_gain,
    norm_shift,
    query_weight,
    query_bias,
    keyval_weight,
    value_bias,
    mixer_weight,
    mixer_bias,
    ffnorm_gain,
    ffnorm_shift,
    up_weight,
    up_bias,
    down_weight,
    down_bias,
):
    y, c, z, x = [lax.axis_index(name) for name in ("y", "c", "z", "x")]
    length = lax.axis_size("z")
    place = y * 2 + c
    slots, seg, width = tokens.shape
    rows = slots * seg
    head_dim = value_bias.shape[0] * 4
    hidden = up_weight.shape[1]
    hidden_block = hidden // (8 * length)
    hidden_mine = hidden // 8
    with_length = 2 * length * seg > MIN_LEN
    scal = jnp.concatenate([jnp.stack([z, x]).astype(jnp.int32), lengths])

    quarter = width // 4
    v_part = value_bias.shape[0]
    v_place = lax.dynamic_update_slice(jnp.zeros((quarter,), BF), value_bias, (place * v_part,))
    small = jnp.stack(
        [norm_gain, norm_shift, query_bias, mixer_bias, ffnorm_gain, ffnorm_shift, down_bias, v_place]
    )
    small = jnp.concatenate([small, jnp.zeros_like(small)], axis=0)

    down_mine = pick(down_weight.reshape(length, 2, hidden_block, width), x, 1).reshape(
        hidden_mine, width
    )
    up_bias_mine = pick(up_bias.reshape(length, 2, hidden_block), x, 1).reshape(1, hidden_mine)
    aligned = hidden_block % 128 == 0
    up_given = up_weight
    if not aligned:
        up_given = pick(up_weight.reshape(quarter, 4, length, 2, hidden_block), x, 3)
        up_given = up_given.reshape(quarter, 4, hidden_mine).transpose(1, 0, 2)

    token_pos = (z * 2 + x) * seg + jnp.arange(seg, dtype=jnp.int32)
    valid = (token_pos[None, :] < lengths[:, None]).astype(F32).reshape(rows, 1)
    d_down = cotangent.reshape(rows, width)
    if with_length:
        d_down = (d_down.astype(F32) * valid).astype(BF)
    d_out = d_down.astype(F32)

    flat = tokens.reshape(rows, width)
    (
        second,
        residual,
        first,
        queries,
        kv_all,
        mixed,
        lse,
        vectors,
        full_query,
        full_mixer,
        full_keyval,
        up_mine,
        down_all,
    ) = front(
        lengths,
        flat,
        small,
        keyval_weight,
        query_weight,
        mixer_weight,
        up_given,
        d_down,
        slots,
        length,
        with_length,
        aligned,
        hidden_mine,
    )
    if aligned and length == 4:
        return finish_fast(
            (
                tokens,
                lengths,
                d_down,
                up_weight,
                down_weight,
                up_bias_mine.astype(F32),
                (y, c, z, x),
                slots,
                length,
                with_length,
            ),
            (second, residual, first, queries, kv_all, mixed, lse, vectors),
            (full_query, full_mixer, full_keyval, up_mine, down_all.reshape(8 * rows, width)),
        )
    inputs = flat.astype(F32)
    gain, ffgain, d_bias = vectors[0:1], vectors[4:5], vectors[6:7]
    unit1, rstd1 = norm_stats(inputs)
    unit2, rstd2 = norm_stats(residual)
    q_t, mixed_t = queries.T, mixed.T

    d_second, out_parts, down_part, up_part, ubias_part = ffn(
        second,
        down_all.reshape(8 * rows, width),
        up_mine,
        up_bias_mine.astype(F32),
        down_mine,
        length,
    )
    output = residual + scatter_plane([out_parts[i] for i in range(4)]) + d_bias
    layer_out = output.astype(BF).reshape(tokens.shape)
    down_grad = scatter_line(down_part.reshape(length, hidden_block, width), z, length)
    ubias_grad = scatter_line(ubias_part.reshape(length, hidden_block), z, length)
    out_rows = width // (8 * length)
    up_sum = scatter_line(up_part, z, length).astype(BF)
    up_rows = lax.all_to_all(
        up_sum.reshape(8, out_rows, hidden_mine), ("y", "c", "x"), 0, 0, tiled=True
    )
    up_grad = (
        up_rows.reshape(4, 2, out_rows, length, hidden_block)
        .transpose(2, 0, 3, 1, 4)
        .reshape(out_rows, hidden)
        .astype(F32)
    )

    d_residual = d_out + norm_backward(d_second, unit2, rstd2, ffgain)
    d_mix = d_residual.astype(BF)
    d_mixed_t = dot(full_mixer, d_mix, ((1,), (1,))).astype(BF)
    where = (y, c, z, x)
    sizes = (length, width)
    mixer_all = scatter_all(
        mixed,
        d_mix,
        (
            jnp.sum(d_mix.astype(F32), axis=0),
            jnp.sum(d_second * unit2, axis=0),
            jnp.sum(d_second, axis=0),
            jnp.sum(d_out, axis=0),
        ),
        where,
        sizes,
    )

    dq_t, dkv = attn_backward(scal, q_t, kv_all, mixed_t, d_mixed_t, lse, 4, with_length)
    dkv = dkv.reshape(slots, length, 2, seg, 2 * head_dim)
    running = None
    for step in range(length - 1, -1, -1):
        term = dkv[:, step]
        term = pick(term, x, 1) + swap(pick(term, 1 - x, 1).astype(BF), "x").astype(F32)
        if running is not None:
            term = term + lax.ppermute(
                running.astype(BF), "z", [(i, i - 1) for i in range(1, length)]
            ).astype(F32)
        running = term
    d_keyvals = running.reshape(rows, 2 * head_dim).astype(BF)
    d_first = dot(dq_t, full_query, ((0,), (1,))) + dot(d_keyvals, full_keyval, ((1,), (1,)))
    tokens_grad = (d_residual + norm_backward(d_first, unit1, rstd1, gain)).astype(BF)
    d_queries = dq_t.T
    devices = 8 * length
    vbias = jnp.sum(d_keyvals[:, head_dim:].astype(F32), axis=0)
    vbias = jnp.pad(
        vbias.reshape(devices, head_dim // devices),
        ((0, 0), (0, out_rows - head_dim // devices)),
    ).reshape(width)
    query_all = scatter_all(
        first,
        jnp.concatenate([d_queries, d_keyvals], axis=1),
        (
            jnp.sum(d_first * unit1, axis=0),
            jnp.sum(d_first, axis=0),
            jnp.sum(d_queries.astype(F32), axis=0),
            vbias,
        ),
        where,
        sizes,
    )
    kv_end = width + 2 * head_dim
    return (
        layer_out,
        tokens_grad.reshape(tokens.shape),
        query_all[:, kv_end],
        query_all[:, kv_end + 1],
        query_all[:, :width],
        query_all[:, kv_end + 2],
        query_all[:, width:kv_end],
        query_all[: head_dim // devices, kv_end + 3],
        mixer_all[:, :width],
        mixer_all[:, width],
        mixer_all[:, width + 1],
        mixer_all[:, width + 2],
        up_grad,
        ubias_grad,
        down_grad,
        mixer_all[:, width + 3],
    )


def solution(mesh):
    ctx = mesh.shape["ctx"]
    fine = Mesh(mesh.devices.reshape(2, 2, ctx // 2, 2), ("y", "c", "z", "x"))
    fsdp, both, every = ("y", "c"), ("z", "x"), ("y", "c", "z", "x")
    return jax.shard_map(
        body,
        mesh=fine,
        in_specs=(
            P(fsdp, both, None),
            P(fsdp),
            P(fsdp, both, None),
            P(fsdp),
            P(fsdp),
            P(fsdp, None),
            P(fsdp),
            P(fsdp, None),
            P(fsdp),
            P(fsdp, None),
            P(fsdp),
            P(fsdp),
            P(fsdp),
            P(fsdp, None),
            P(fsdp),
            P(fsdp, None),
            P(fsdp),
        ),
        out_specs=(
            P(fsdp, both, None),
            P(fsdp, both, None),
            P(every),
            P(every),
            P(every, None),
            P(every),
            P(every, None),
            P(every),
            P(every, None),
            P(every),
            P(every),
            P(every),
            P(every, None),
            P(every),
            P(every, None),
            P(every),
        ),
        check_vma=False,
    )
```

profile of v0, /device:TPU:0, one launch (start us, length us, event | category | flops | bytes accessed | tf_op | source)
XLA Modules:
  0.0 463.0 jit_solution(16639038784171383827)
XLA Ops:
  0.7 0.8 dynamic_update_slice.4
  1.5 0.7 stack.24
  2.1 0.7 stack.25
  2.8 0.7 stack.26
  3.5 0.7 stack.27
  4.2 0.7 stack.28
  4.9 0.7 stack.29
  5.6 0.7 stack.30
  6.2 1.2 concatenate.3.smalls_ref
  7.5 0.0 copy-start.7
  7.5 115.8 %shard_map.288 = (bf16[256,2048]{1,0:T(8,128)(2,1)}, f32[256,2048]{1,0:T(8,128)}, bf16[256,2048]{1,0:T(8,128)(2,1)}, bf16[256,2048]{1,0:T(8,128)(2,1)}, bf16[2,4...) custom-call(s32[2]{0:T(128)} %lengths_ref.3, ...), custom_call_target="tpu_custom_call" | custom-call | flops 6442450944 | bytes 41943040 | tf_op jit(solution)/shard_map/pallas_call | solution.py:1036
  123.3 0.0 copy-done.7
  123.3 0.6 convert.5.ubias_ref
  123.9 108.5 %shard_map.289 = (f32[256,2048]{1,0:T(8,128)}, bf16[4,256,2048]{2,1,0:T(8,128)(2,1)}, bf16[1024,2048]{1,0:T(8,128)(2,1)}, bf16[4,256,2048]{2,1,0:T(8,128)(2,1)}, f32[1,1024]{1,0:T(1,128)}, /*index=5*/f32[8,2048]{1,0:T(8,128)}) custom-call(bf16[256,2048]{1,0:T(8,128)(2,1)} %get-tuple-element.44.second_ref, bf16[256,2048]{1,0:T(8,128)(2,1)} %bitcast.50, ...), custom_call_target="tpu_custom_call" | custom-call | flops 51539607552 | bytes 41943040 | tf_op jit(solution)/shard_map/pallas_call | solution.py:1388
  232.5 215.6 %shard_map.290 = (bf16[256,2048]{1,0:T(8,128)(2,1)}, f32[64,2304]{1,0:T(8,128)}, f32[64,2048]{1,0:T(8,128)}, bf16[64,8192]{1,0:T(8,128)(2,1)}, f32[16,2048]{1,0:...) custom-call(s32[2]{0:T(128)} %lengths_ref.3, bf16[256,2048]{1,0:T(8,128)(2,1)} %bitcast.52, ...), custom_call_target="tpu_custom_call" | custom-call | flops 12884901888 | bytes 41943040 | tf_op jit(solution)/shard_map/pallas_call | solution.py:2084
  448.1 0.0 copy-start.2
  448.1 0.0 copy-start.1
  448.1 3.9 add_bitcast_fusion
  452.0 0.0 copy-start
  452.0 0.0 copy-done.2
  452.0 1.5 convert_element_type.58
  453.4 1.1 slice.57
  454.5 0.0 copy-done.1
  454.5 0.1 copy-done
  454.6 0.0 copy-start.4
  454.6 0.0 copy-start.6
  454.6 3.1 fusion
  457.7 0.0 copy-start.3
  457.7 0.0 copy-start.5
  457.7 0.0 copy-done.4
  457.7 0.8 slice.65
  458.6 0.0 copy-done.6
  458.6 0.1 constant_dynamic-slice_fusion.2
  458.7 0.5 slice_bitcast_fusion
  459.2 0.6 slice.67
  459.9 0.6 fusion.1
  460.4 0.6 constant_dynamic-slice_fusion
  461.0 0.0 copy-done.3
  461.0 1.0 copy.36
  462.0 0.0 copy-done.5
  462.0 0.8 copy.37
  (6 shorter events, 0.1 us)
Async XLA Ops:
  7.5 115.8 %copy-start.7 = (bf16[2048]{0:T(1024)(128)(2,1)S(1)}, bf16[2048]{0:T(1024)(128)(2,1)}, u32[]{:S(2)}) copy-start(bf16[2048]{0:T(1024)(128)(2,1)} %param.31) | copy-start | bytes 12292
  448.1 3.9 copy-start.2
  448.1 6.4 %copy-start.1 = (f32[256,2048]{1,0:T(8,128)S(1)}, f32[256,2048]{1,0:T(8,128)}, u32[]{:S(2)}) copy-start(f32[256,2048]{1,0:T(8,128)} %get-tuple-element.42.residual_ref) | copy-start | bytes 6291460
  452.0 2.6 copy-start
  454.6 3.1 copy-start.4
  454.6 3.9 copy-start.6
  457.7 3.3 copy-start.3
  457.7 4.3 copy-start.5
where the time goes:
time: 469 us; the launch traced here: 463 us
  Pallas kernels  440 us (94%)
  local copies, waits for them, and re-layouts  13 us (3%)
  other arithmetic  9.02 us (2%)
    pallas_call x1, Pallas kernels, back(): pl.pallas_call(functools.partial(back_kernel, length=length, slots=slots,...  216 us
    pallas_call x1, Pallas kernels, front(): pl.pallas_call(functools.partial(front_kernel, length=length, slots=slots...  116 us
    pallas_call x1, Pallas kernels, feed(): pl.pallas_call(functools.partial(feed_kernel, length=length), in_specs=[h...  109 us

commit v1 on v0

--- a/solution.py
+++ b/solution.py
@@ -630,47 +630,28 @@
         return pltpu.make_async_copy(self.shard, self.full.at[pl.ds(start, self.rows)], sem)
 
 
-class WeightStep:
-    def __init__(self, weight, i):
-        self.weight, self.i = weight, i
-
-    def start(self, begin):
-        begin(self.weight.over_y(self.i))
-
-    def arrive(self):
-        self.weight.over_y(self.i).wait_recv()
-
-    def follow(self, begin):
-        begin(self.weight.over_x(self.i))
-        begin(self.weight.over_c(self.i, 0))
-
-    def late(self, begin):
-        self.weight.over_x(self.i).wait_recv()
-        begin(self.weight.over_c(self.i, 1))
-
-
-class Stream:
+class Arrivals:
     def __init__(self, order, begin):
         self.order, self.begin = order, begin
         self.next = 0
         self.behind = None
-        for step in order[:2]:
-            step.start(begin)
 
     def event(self):
-        n = self.next
+        if self.next == len(self.order):
+            return
+        weight, i = self.order[self.next]
         self.next += 1
-        step = self.order[n]
-        step.arrive()
-        if n + 2 < len(self.order):
-            self.order[n + 2].start(self.begin)
-        step.follow(self.begin)
+        weight.over_y(i).wait_recv()
+        self.begin(weight.over_x(i))
+        self.begin(weight.over_c(i, 0))
         self.late()
-        self.behind = step
+        self.behind = (weight, i)
 
     def late(self):
         if self.behind is not None:
-            self.behind.late(self.begin)
+            weight, i = self.behind
+            weight.over_x(i).wait_recv()
+            self.begin(weight.over_c(i, 1))
         self.behind = None
 
 
@@ -803,36 +784,22 @@
             device_id_type=MESH,
         )
 
-    class UpStep:
-        def start(self, begin):
-            for copy in up_far:
-                begin(copy)
-
-        def arrive(self):
-            for copy in up_far:
-                copy.wait_recv()
-
-        def follow(self, begin):
-            for target in range(length):
-                @pl.when(target != z)
-                def share():
-                    for k in range(2):
-                        up_share(k, z, target).start()
-
-        def late(self, begin):
-            pass
-
-    stream = Stream(
-        [WeightStep(query_w, i) for i in range(4)] + [UpStep()] + [WeightStep(mixer_w, i) for i in range(4)],
-        begin,
-    )
-    for weight in weights:
-        begin(weight.own_c())
+    same, other_half = pl.ds(0, rows), pl.ds(rows, rows)
+    for copy in up_far:
+        begin(copy)
+    for i in range(4):
+        begin(query_w.over_y(i))
+    for i in range(4):
+        begin(mixer_w.over_y(i))
+    cot_y = begin(remote(cot_ref, cots_out.at[2, same], c_send, c_recv, 1, to_y))
+    cot_x = begin(remote(cot_ref, cots_out.at[1, same], c_send, c_recv, 0, to_x))
+    stream = Arrivals([(query_w, i) for i in range(4)] + [(mixer_w, i) for i in range(4)], begin)
+    begin(query_w.own_c())
 
     for copy in small_copies:
         copy.wait_recv()
     locals_[3].wait()
-    vec_v[...] = jnp.concatenate([smalls_v[f].astype(F32) for f in range(4)], axis=1)
+    vec_v[...] = jnp.concatenate([smalls_v[f] for f in range(4)], axis=1)
 
     def first_norm(span):
         unit, _ = norm_rows(tokens_v[span, :].astype(F32))
@@ -843,7 +810,6 @@
     kv_far.wait_recv()
     far_rows = wkv_v.at[pl.ds(pl.multiple_of((place ^ 2) * quarter, quarter), quarter)]
     kv_pass = begin(remote(far_rows, far_rows, s_send, s_recv, 5, sib))
-    stream.event()
     kv_near.wait_recv()
     locals_[2].wait()
     kv_pass.wait_recv()
@@ -880,30 +846,34 @@
             def onward():
                 kv_up(t + 1).start()
 
+    for t in range(length):
+        kv_step(t)
+    for copy in up_far:
+        copy.wait_recv()
+    for target in range(length):
+        @pl.when(target != z)
+        def share():
+            for k in range(2):
+                up_share(k, z, target).start()
+
+    while stream.next < 4:
+        stream.event()
+
+    top, bottom = pl.ds(0, rows // 2), pl.ds(rows // 2, rows // 2)
+    if not aligned:
+        cot_local = pltpu.make_async_copy(cot_ref, cots_out.at[0, same], local_sem.at[4])
+        cot_local.start()
+    cot_share = [
+        remote(cot_ref if k == 0 else cots_out.at[k, same], cots_out.at[k, other_half], c_send, c_recv, 2 + k, sib)
+        for k in range(3 if aligned else 4)
+    ]
+
     for copy in up_local:
         copy.start()
     for copy in up_near:
         begin(copy)
-
-    for t in range(length):
-        kv_step(t)
-        if t < 3:
-            stream.event()
-
-    same, other_half = pl.ds(0, rows), pl.ds(rows, rows)
-    top, bottom = pl.ds(0, rows // 2), pl.ds(rows // 2, rows // 2)
-    if not aligned:
-        cot_local = pltpu.make_async_copy(cot_ref, cots_out.at[0, same], local_sem.at[4])
-        cot_local.start()
-    cot_x = remote(cot_ref, cots_out.at[1, same], c_send, c_recv, 0, to_x)
-    cot_y = remote(cot_ref, cots_out.at[2, same], c_send, c_recv, 1, to_y)
-    cot_share = [
-        remote(cot_ref if k == 0 else cots_out.at[k, same], cots_out.at[k, other_half], c_send, c_recv, 2 + k, sib)
-        for k in range(4)
-    ]
-    cot_dx = remote(cots_out.at[2, top], cots_out.at[3, top], c_send, c_recv, 6, to_x)
-    cot_dy = remote(cots_out.at[1, bottom], cots_out.at[3, bottom], c_send, c_recv, 7, to_y)
-
+    begin(mixer_w.own_c())
+    begin(cot_share[0])
     stream.late()
     locals_[0].wait()
     query_w.settle()
@@ -974,12 +944,7 @@
     for s in range(slots):
         for g in range(heads // group):
             attend(s, g)
-            if stream.next < len(stream.order):
-                stream.event()
-                if stream.next == len(stream.order) - 1:
-                    begin(cot_x)
-                    begin(cot_y)
-                    begin(cot_share[0])
+            stream.event()
 
     stream.late()
     locals_[1].wait()
@@ -1004,12 +969,12 @@
     begin(cot_share[1])
     begin(cot_share[2])
     if not aligned:
-        begin(cot_dx)
-        begin(cot_dy)
+        cot_dx = begin(remote(cots_out.at[2, top], cots_out.at[3, top], c_send, c_recv, 6, to_x))
+        cot_dy = begin(remote(cots_out.at[1, bottom], cots_out.at[3, bottom], c_send, c_recv, 7, to_y))
         cot_dx.wait_recv()
         cot_dy.wait_recv()
         begin(cot_share[3])
-    for copy in cot_share[: 3 if aligned else 4] + up_near:
+    for copy in cot_share + up_near:
         copy.wait_recv()
     for copy in up_local:
         copy.wait()
@@ -1047,7 +1012,7 @@
             jax.ShapeDtypeStruct((slots, length, 2 * seg, both), BF),
             jax.ShapeDtypeStruct((rows, width), BF),
             jax.ShapeDtypeStruct((slots, groups, 1, 4 * seg), F32),
-            jax.ShapeDtypeStruct((16, width), F32),
+            jax.ShapeDtypeStruct((8, width), F32),
             jax.ShapeDtypeStruct((width, width), BF),
             jax.ShapeDtypeStruct((width, width), BF),
             jax.ShapeDtypeStruct((width, both), BF),
@@ -1057,7 +1022,7 @@
         scratch_shapes=[
             pltpu.VMEM((width, width), BF),
             pltpu.VMEM((width, width), BF),
-            pltpu.VMEM((4, 16, width // 4), BF),
+            pltpu.VMEM((4, 8, width // 4), F32),
             sems((7,)),
             sems((34,)),
             sems((34,)),
@@ -1097,6 +1062,7 @@
     up_part_ref,
     ubias_part_ref,
     vsum_ref,
+    first_ref,
     tokens_v,
     cots_v,
     up_v,
@@ -1105,11 +1071,11 @@
     dupper_v,
     sib_out,
     sib_in,
-    red_in,
     chip_out,
     chip_in,
     acc_v,
     stage_v,
+    credit,
     load_sem,
     stage_sem,
     gs_send,
@@ -1123,13 +1089,13 @@
     hidden = up_ref.shape[1]
     half = rows // 2
     chunk = 2 * rows
-    y, c, x = [lax.axis_index(name) for name in ("y", "c", "x")]
+    y, c, z, x = [lax.axis_index(name) for name in ("y", "c", "z", "x")]
     sib, to_x, to_y = {"c": 1 - c}, {"x": 1 - x}, {"y": 1 - y}
     diag = {"x": 1 - x, "y": 1 - y}
     chips = (None, to_x, to_y, diag)
 
     loads = [
-        pltpu.make_async_copy(second_ref, tokens_v.at[0, pl.ds(0, rows)], load_sem.at[0]),
+        pltpu.make_async_copy(second_ref, tokens_v.at[pl.ds(0, rows)], load_sem.at[0]),
         pltpu.make_async_copy(cot_ref, cots_v.at[pl.ds(0, rows)], load_sem.at[1]),
         pltpu.make_async_copy(
             down_all_ref.at[pl.ds(rows, 5 * rows)], cots_v.at[pl.ds(rows, 5 * rows)], load_sem.at[2]
@@ -1162,16 +1128,24 @@
     ]
     for load in loads + downs_in + ups_in:
         load.start()
-    greet((sib, to_x, to_y, diag))
+    barrier = pltpu.get_barrier_semaphore()
+    for device in (sib, to_x, to_y, diag):
+        pl.semaphore_signal(barrier, inc=1, device_id=device, device_id_type=MESH)
+    for step in (-1, 1):
+        @pl.when((z + step >= 0) & (z + step < length))
+        def hello():
+            pl.semaphore_signal(barrier, inc=1, device_id={"z": z + step}, device_id_type=MESH)
+    inner = (z > 0).astype(jnp.int32) + (z < length - 1).astype(jnp.int32)
+    pl.semaphore_wait(barrier, 4 + inner)
     loads[0].wait()
 
-    same, other = pl.ds(0, rows), pl.ds(rows, rows)
-    top, bottom = pl.ds(0, half), pl.ds(half, half)
+    same, other = (0, rows), (rows, rows)
+    top, bottom = (0, half), (half, half)
 
     def gather(index, chip, span_src, chip_dst, span_dst, device):
-        return remote(
-            tokens_v.at[chip, span_src], tokens_v.at[chip_dst, span_dst], gs_send, gs_recv, index, device
-        )
+        src = tokens_v.at[pl.ds(chip * chunk + span_src[0], span_src[1])]
+        dst = tokens_v.at[pl.ds(chip_dst * chunk + span_dst[0], span_dst[1])]
+        return remote(src, dst, gs_send, gs_recv, index, device)
 
     send_x = gather(0, 0, same, 1, same, to_x)
     send_y = gather(1, 0, same, 2, same, to_y)
@@ -1193,13 +1167,9 @@
     cot_dx = remote(cot_part(2, 0, half), cot_part(3, 0, half), gs_send, gs_recv, 8, to_x)
     cot_dy = remote(cot_part(1, half, half), cot_part(3, half, half), gs_send, gs_recv, 9, to_y)
     cot_dc = remote(cot_part(3, 0, rows), cot_part(3, rows, rows), gs_send, gs_recv, 10, sib)
-    cot_dx.start()
-    cot_dy.start()
 
     def grad_active(span, index):
-        @tiles(hidden // 512, 512)
-        def columns(cols, _):
-            dupper_v[span, cols] = dot(cots_v[span, :], down_v[cols, :], ((1,), (1,))).astype(BF)
+        dupper_v[span, :] = dot(cots_v[span, :], down_v[...], ((1,), (1,))).astype(BF)
 
     @pl.loop(0, 3)
     def near_grads(k):
@@ -1209,13 +1179,18 @@
         load.wait()
 
     def chip_work(k):
-        @tiles(hidden // 256, 256)
+        block = pl.ds(k * chunk, chunk)
+
+        @tiles(hidden // 512, 512)
         def columns(cols, _):
-            block = pl.ds(k * chunk, chunk)
-            upper = dot(tokens_v[k], up_v[:, cols]) + ubias_ref[:, cols]
-            active, slope = gelu_pair(upper)
-            active_v[block, cols] = active.astype(BF)
-            d_upper = (dupper_v[block, cols].astype(F32) * slope).astype(BF)
+            if k < 3:
+                upper = dot(tokens_v[block, :], up_v[:, cols]) + ubias_ref[:, cols]
+                active, slope = gelu_pair(upper)
+                active_v[block, cols] = active.astype(BF)
+                d_upper = (dupper_v[block, cols].astype(F32) * slope).astype(BF)
+            else:
+                d_active = dot(cots_v[block, :], down_v[cols, :], ((1,), (1,)))
+                d_upper = (d_active * dupper_v[block, cols].astype(F32)).astype(BF)
             dupper_v[block, cols] = d_upper
             part = jnp.sum(d_upper.astype(F32), axis=0, keepdims=True)
             if k == 0:
@@ -1223,18 +1198,18 @@
             else:
                 ubias_part_ref[:, cols] += part
 
-        @tiles(width // 512, 512)
+        theirs, mine = pl.ds(k * chunk + rows, rows), pl.ds(k * chunk, rows)
+
+        @tiles(width // 1024, 1024)
         def to_sibling(cols, _):
-            sib_out[k, :, cols] = dot(
-                dupper_v[pl.ds(k * chunk + rows, rows), :], up_v[cols, :], ((1,), (1,))
-            ).astype(BF)
+            sib_out[k, :, cols] = dot(dupper_v[theirs, :], up_v[cols, :], ((1,), (1,))).astype(BF)
 
         pair = remote(sib_out.at[k], sib_in.at[k], rs_send, rs_recv, k, sib)
         pair.start()
 
-        @tiles(width // 512, 512)
+        @tiles(width // 1024, 1024)
         def keep(cols, _):
-            dres_ref[:, cols] = dot(dupper_v[pl.ds(k * chunk, rows), :], up_v[cols, :], ((1,), (1,)))
+            dres_ref[:, cols] = dot(dupper_v[mine, :], up_v[cols, :], ((1,), (1,)))
 
         pair.wait_recv()
 
@@ -1260,6 +1235,8 @@
     send_y.wait_recv()
     share[2].start()
     diag_x.start()
+    cot_dx.start()
+    cot_dy.start()
     share[1].wait_recv()
     sent += chip_work(1)
     share[2].wait_recv()
@@ -1267,94 +1244,111 @@
     diag_x.wait_recv()
     diag_y.wait_recv()
     share[3].start()
+    share[3].wait_recv()
+
+    @tiles(hidden // 512, 512)
+    def last_slopes(cols, _):
+        block = pl.ds(3 * chunk, chunk)
+        upper = dot(tokens_v[block, :], up_v[:, cols]) + ubias_ref[:, cols]
+        active, slope = gelu_pair(upper)
+        active_v[block, cols] = active.astype(BF)
+        dupper_v[block, cols] = slope.astype(BF)
+
     cot_dx.wait_recv()
     cot_dy.wait_recv()
     cot_dc.start()
     cot_dc.wait_recv()
-    grad_active(pl.ds(3 * chunk, chunk), 3)
-    share[3].wait_recv()
-    sent += chip_work(3)
-
-    def staged(slot, value, target):
-        stage_v[slot] = value.astype(BF)
-        copy = pltpu.make_async_copy(stage_v.at[slot], target, stage_sem.at[slot])
-        copy.start()
-        return copy
-
-    pairs = []
-    for k in range(4):
-        sent[0 if k == 0 else 2 * k - 1].wait_send()
-
-        @tiles(width // 512, 512)
-        def to_sibling(cols, _):
-            sib_out[k, :, cols] = dot(
-                active_v[pl.ds(k * chunk + rows, rows), :], down_v[:, cols]
-            ).astype(BF)
-
-        pair = remote(sib_out.at[k], red_in.at[k], rs_send, rs_recv, 7 + k, sib)
-        pair.start()
-        pairs.append(pair)
-
-    for k in range(4):
-
-        @tiles(width // 512, 512)
-        def keep(cols, _):
-            dres_ref[:, cols] = dot(active_v[pl.ds(k * chunk, rows), :], down_v[:, cols])
-
-        pairs[k].wait_recv()
-
-        def total(span):
-            red_in[k, span, :] = (dres_ref[span, :] + red_in[k, span, :].astype(F32)).astype(BF)
-
-        for_rows(rows, total)
-    red_copy = pltpu.make_async_copy(red_in, red_ref, load_sem.at[3])
-    red_copy.start()
-
-    @pl.loop(0, hidden // 512)
-    def downs(r):
-        block = pl.ds(pl.multiple_of(r * 512, 512), 512)
+
+    @pl.loop(0, 2)
+    def downs(n):
+        block = pl.ds(pl.multiple_of(n * 512, 512), 512)
         copies = []
-        for j in range(width // 512):
-            cols = pl.ds(j * 512, 512)
-            copies.append(
-                staged(
-                    j,
-                    dot(active_v[:, block], cots_v[:, cols], ((0,), (0,))),
-                    down_part_ref.at[block, cols],
-                )
+        for m in range(2):
+            cols = pl.ds(m * (width // 2), width // 2)
+            stage_v[m] = dot(active_v[:, block], cots_v[:, cols], ((0,), (0,))).astype(BF)
+            copy = pltpu.make_async_copy(
+                stage_v.at[m], down_part_ref.at[block, cols], stage_sem.at[m * length]
             )
+            copy.start()
+            copies.append(copy)
         for copy in copies:
             copy.wait()
 
+    line_block = hidden // length
+    ends = []
+    for n in range(2):
+        for way, device in ((0, {"z": z + 1}), (1, {"z": z - 1})):
+            b = length - 1 if way == 0 else 0
+            part = down_part_ref.at[pl.ds(b * line_block, line_block)] if n else up_part_ref.at[b]
+            ends.append(remote(part, first_ref.at[n, way], rs_send, rs_recv, 11 + 2 * n + way, device))
+
+    def send_ends(n):
+        for way, edge in ((0, 0), (1, length - 1)):
+            @pl.when(z == edge)
+            def send_end():
+                ends[2 * n + way].start()
+
+    send_ends(1)
+    sent += chip_work(3)
+
+    pl.semaphore_signal(credit, inc=1, device_id=sib, device_id_type=MESH)
+    pl.semaphore_wait(credit, 1)
+
     piece = quarter // length
 
-    @pl.loop(0, hidden // 512)
-    def ups(r):
-        first = pl.multiple_of(r * 512, 512)
-        cols = pl.ds(first, 512)
+    @pl.loop(0, 2)
+    def ups(lane_half):
+        lanes = pl.ds(pl.multiple_of(lane_half * hidden, hidden), hidden)
         copies = []
-        for f in range(4):
-            value = None
-            for k in range(4):
-                term = dot(
-                    tokens_v[k, :, f * quarter : (f + 1) * quarter],
-                    dupper_v[k * chunk : (k + 1) * chunk, cols],
-                    ((0,), (0,)),
-                )
-                value = term if value is None else value + term
-            stage_v[f] = value.astype(BF)
+        for n in range(2):
+            cols = pl.ds(pl.multiple_of((lane_half * 2 + n) * quarter, quarter), quarter)
+            stage_v[n] = dot(tokens_v[:, cols], dupper_v[...], ((0,), (0,))).astype(BF)
             for level in range(length):
                 copy = pltpu.make_async_copy(
-                    stage_v.at[f, pl.ds(level * piece, piece)],
-                    up_part_ref.at[
-                        level, pl.ds((f % 2) * piece, piece), pl.ds((f // 2) * hidden + first, 512)
-                    ],
-                    stage_sem.at[4 + f * length + level],
+                    stage_v.at[n, pl.ds(level * piece, piece)],
+                    up_part_ref.at[level, pl.ds(n * piece, piece), lanes],
+                    stage_sem.at[n * length + level],
                 )
                 copy.start()
                 copies.append(copy)
         for copy in copies:
             copy.wait()
+
+    send_ends(0)
+
+    for k in range(4):
+        sent[0 if k == 0 else 2 * k - 1].wait_send()
+
+    def out_pair(k):
+        return remote(sib_out.at[k], sib_in.at[k], rs_send, rs_recv, 7 + k, sib)
+
+    @pl.loop(0, 4)
+    def outs_away(k):
+        theirs = pl.ds(pl.multiple_of(k * chunk + rows, rows), rows)
+
+        @tiles(width // 1024, 1024)
+        def columns(cols, _):
+            sib_out[k, :, cols] = dot(active_v[theirs, :], down_v[:, cols]).astype(BF)
+
+        out_pair(k).start()
+
+    @pl.loop(0, 4)
+    def outs_here(k):
+        mine = pl.ds(pl.multiple_of(k * chunk, rows), rows)
+
+        @tiles(width // 1024, 1024)
+        def columns(cols, _):
+            dres_ref[:, cols] = dot(active_v[mine, :], down_v[:, cols])
+
+        out_pair(k).wait_recv()
+
+        def total(span):
+            sib_in[k, span, :] = (dres_ref[span, :] + sib_in[k, span, :].astype(F32)).astype(BF)
+
+        for_rows(rows, total)
+
+    red_copy = pltpu.make_async_copy(sib_in, red_ref, load_sem.at[3])
+    red_copy.start()
 
     for k in range(3):
         remote(chip_out.at[k], chip_in.at[k], rs_send, rs_recv, 4 + k, chips[k + 1]).wait_recv()
@@ -1375,7 +1369,19 @@
 
     for_rows(rows, norm_back)
     red_copy.wait()
-    for copy in [send_x, send_y, diag_x, diag_y, cot_dx, cot_dy, cot_dc] + share + pairs + sent[2::2]:
+    for n in range(2):
+        for way, edge in ((0, 0), (1, length - 1)):
+            @pl.when(z == edge)
+            def end_sent():
+                ends[2 * n + way].wait_send()
+
+            @pl.when(z == (1 if way == 0 else length - 2))
+            def end_here():
+                ends[2 * n + way].wait_recv()
+
+    for k in range(4):
+        out_pair(k).wait_send()
+    for copy in [send_x, send_y, diag_x, diag_y, cot_dx, cot_dy, cot_dc] + share + sent[2::2]:
         copy.wait_send()
 
 
@@ -1388,7 +1394,7 @@
     return pl.pallas_call(
         functools.partial(feed_kernel, length=length),
         in_specs=[hbm, hbm, hbm, hbm, hbm, vmem, vmem, vmem, hbm],
-        out_specs=[vmem, hbm, hbm, hbm, vmem, vmem],
+        out_specs=[vmem, hbm, hbm, hbm, vmem, vmem, hbm],
         out_shape=[
             jax.ShapeDtypeStruct((rows, width), F32),
             jax.ShapeDtypeStruct((4, rows, width), BF),
@@ -1396,9 +1402,10 @@
             jax.ShapeDtypeStruct((length, hidden // length, width), BF),
             jax.ShapeDtypeStruct((1, hidden), F32),
             jax.ShapeDtypeStruct((8, width), F32),
+            jax.ShapeDtypeStruct((2, 2, hidden // length, width), BF),
         ],
         scratch_shapes=[
-            pltpu.VMEM((4, 2 * rows, width), BF),
+            pltpu.VMEM((8 * rows, width), BF),
             pltpu.VMEM((8 * rows, width), BF),
             pltpu.VMEM((width, hidden), BF),
             pltpu.VMEM((hidden, width), BF),
@@ -1406,17 +1413,17 @@
             pltpu.VMEM((8 * rows, hidden), BF),
             pltpu.VMEM((4, rows, width), BF),
             pltpu.VMEM((4, rows, width), BF),
-            pltpu.VMEM((4, rows, width), BF),
             pltpu.VMEM((3, rows, width), BF),
             pltpu.VMEM((3, rows, width), BF),
             pltpu.VMEM((rows, width), F32),
-            pltpu.VMEM((4, 512, 512), BF),
+            pltpu.VMEM((2, 512, 1024), BF),
+            pltpu.SemaphoreType.REGULAR,
             sems((7 + 2 * length,)),
-            sems((4 + 4 * length,)),
+            sems((2 * length,)),
             sems((11,)),
             sems((11,)),
-            sems((11,)),
-            sems((11,)),
+            sems((15,)),
+            sems((15,)),
         ],
         compiler_params=pltpu.CompilerParams(
             collective_id=4, has_side_effects=True, vmem_limit_bytes=62 << 20
@@ -1443,9 +1450,11 @@
 
 
 class LineSum:
-    def __init__(self, links, z, length, parts, landing):
+    def __init__(self, links, z, length, parts, landing, source=None, given=None):
         self.z, self.length, self.parts, self.landing = z, length, parts, landing
-        self.copies = {}
+        self.source = parts if source is None else source
+        self.given = given
+        self.copies, self.indices = {}, {}
         self.links = links
 
     def position(self, way):
@@ -1464,30 +1473,40 @@
                 ref = self.landing(way, last)
                 ref[...] = jnp.zeros(ref.shape, ref.dtype)
 
-    def step(self, t):
-        if t > 1:
-            self.settle(t - 1)
+    def direct(self, t, ways=(0, 1)):
+        for way in ways:
+            device = {"z": self.z + (1 if way == 0 else -1)}
+            index = self.links.used
+            copy = self.links.copy(
+                self.source.at[self.block(way, t)], self.landing(way, t), device
+            )
+            self.copies[way, t] = copy
+            self.indices[way, t] = index
+
+            @pl.when(self.position(way) == 0)
+            def first():
+                copy.start()
+
+    def onward(self, t):
         for way in range(2):
             pos = self.position(way)
             device = {"z": self.z + (1 if way == 0 else -1)}
-            part = self.parts.at[self.block(way, t)]
-            index = self.links.used
-            direct = self.links.copy(part, self.landing(way, t), device)
-            self.copies[way, t] = direct
-
-            @pl.when(pos == 0)
-            def first():
-                direct.start()
-
-            if t > 1:
-                ref = self.landing(way, t - 1)
-                passed = self.links.again(ref, self.landing(way, t), device, index)
-
-                @pl.when((pos >= 1) & (pos <= t - 1))
-                def onward():
+            ref = self.landing(way, t - 1)
+            passed = self.links.again(ref, self.landing(way, t), device, self.indices[way, t])
+
+            @pl.when((pos >= 1) & (pos <= t - 1))
+            def add():
+                if t == 2 and self.given is not None:
+                    self.given[way].wait()
+                else:
                     self.copies[way, t - 1].wait_recv()
-                    add_rows(ref, part)
-                    passed.start()
+                add_rows(ref, self.parts.at[self.block(way, t)])
+                passed.start()
+
+    def step(self, t):
+        self.direct(t)
+        if t > 1:
+            self.onward(t)
 
     def finish(self, own, out):
         last = self.length - 1
@@ -1514,7 +1533,8 @@
                 self.copies[way, t].wait_send()
 
     def drain(self):
-        self.settle(self.length - 1)
+        for t in range(1 if self.given is None else 2, self.length):
+            self.settle(t)
 
 
 def add_rows(ref, term):
@@ -1548,17 +1568,12 @@
         ) = bufs
         self.links = links
         self.sent = []
+        self.left_copy = self.sum_copy = None
 
     def begin(self, copy):
         copy.start()
         self.sent.append(copy)
         return copy
-
-    def all_cols(self, ref):
-        return ref.at[..., pl.ds(0, self.cols)] if ref.shape[-1] != self.cols else ref
-
-    def half_cols(self, ref):
-        return ref.at[..., pl.ds(0, self.half)] if ref.shape[-1] != self.half else ref
 
     def share(self):
         quarter = self.width // 4
@@ -1575,10 +1590,34 @@
                         ]
         sib = {"c": 1 - self.c}
         self.left_copy = self.begin(self.links.copy(self.left_out, self.left_in, sib))
-        self.right_copy = self.begin(self.links.copy(self.right, self.all_cols(self.right_in), sib))
+        self.share_right()
+
+    def share_right(self):
+        sib = {"c": 1 - self.c}
+        self.right_copy = self.begin(self.links.copy(self.right, self.right_in, sib))
+
+    def share_sums(self, sums, own, out, landing):
+        self.sum_own, self.sum_in = own, landing
+        quarter = self.width // 4
+        block = quarter // (2 * self.length)
+        for core, target in ((1 - self.c, out), (self.c, own)):
+            for y_part in range(2):
+                lanes = pl.ds(pl.multiple_of((y_part * 2 + core) * quarter, quarter), quarter)
+                filler = jnp.zeros((own.shape[2] - sums.shape[0], quarter), F32)
+                turned = jnp.concatenate([sums[:, lanes], filler], axis=0).T.astype(BF)
+                for x_part in range(2):
+                    for level in range(self.length):
+                        start = (level * 2 + x_part) * block
+                        target[y_part * 2 + x_part, level * block : (level + 1) * block, :] = turned[
+                            start : start + block
+                        ]
+        self.sum_copy = self.begin(self.links.copy(out, landing, {"c": 1 - self.c}))
 
     def term(self, y_part, x_part, cols):
         g = y_part * 2 + x_part
+        if cols.start >= self.right.shape[1]:
+            total = self.sum_own[g].astype(F32) + self.sum_in[g].astype(F32)
+            return jnp.concatenate([total, jnp.zeros((total.shape[0], cols.size - total.shape[1]), F32)], axis=1)
         return dot(self.left_own[g], self.right[:, cols]) + dot(self.left_in[g], self.right_in[:, cols])
 
     def columns(self, side, fn):
@@ -1588,8 +1627,11 @@
             fn(pl.ds(side * self.half + j * size, size), pl.ds(j * size, size))
 
     def first(self):
-        self.left_copy.wait_recv()
+        if self.left_copy is not None:
+            self.left_copy.wait_recv()
         self.right_copy.wait_recv()
+        if self.sum_copy is not None:
+            self.sum_copy.wait_recv()
         for n in range(2):
 
             def over_y(cols, local):
@@ -1602,7 +1644,7 @@
             self.columns(1, over_x)
         self.copies1 = [
             self.begin(
-                self.links.copy(self.half_cols(self.send1.at[side]), self.half_cols(self.recv1.at[side]), device)
+                self.links.copy(self.send1.at[side], self.recv1.at[side], device)
             )
             for side, device in ((0, {"y": 1 - self.y}), (1, {"x": 1 - self.x}))
         ]
@@ -1629,7 +1671,7 @@
         self.columns(1, b_out)
         self.copies2 = [
             self.begin(
-                self.links.copy(self.half_cols(self.send2.at[side]), self.half_cols(self.recv2.at[side]), device)
+                self.links.copy(self.send2.at[side], self.recv2.at[side], device)
             )
             for side, device in ((0, {"x": 1 - self.x}), (1, {"y": 1 - self.y}))
         ]
@@ -1650,13 +1692,13 @@
 
             self.columns(side, add)
         rows = pl.ds(pl.multiple_of(self.z * block, block), block)
-        out[...] = self.all_cols(self.hold)[rows, :]
+        out[...] = self.hold[rows, :]
         self.line = LineSum(
             self.links,
             self.z,
             self.length,
-            self.all_cols(self.zpart),
-            lambda way, t: self.all_cols(self.zland.at[way, t - 1]),
+            self.zpart,
+            lambda way, t: self.zland.at[way, t - 1],
         )
 
     def finish(self, out):
@@ -1670,9 +1712,7 @@
 
 def back_kernel(
     lengths_ref,
-    tokens_v,
     dres_ref,
-    first_ref,
     q_ref,
     kv_ref,
     mixed_ref,
@@ -1681,16 +1721,20 @@
     wkv_ref,
     vsum_ref,
     ubias_ref,
+    tokens_ref,
+    first_ref,
     wq_ref,
     wm_ref,
     red_ref,
     down_part,
     up_part,
+    first_ref_z,
     tgrad_ref,
     query_ref,
+    keyval_ref,
     mixer_ref,
     up_ref,
-    vectors_ref,
+    ubias_out,
     far_ref,
     down_last,
     w_v,
@@ -1709,8 +1753,12 @@
     last_v,
     upsend_v,
     uprecv_v,
-    vsend_v,
-    vrecv_v,
+    sums_v,
+    s_own,
+    s_out,
+    s_in,
+    ub_part,
+    ub_land,
     left_own,
     left_out,
     left_in,
@@ -1722,6 +1770,17 @@
     hold,
     zpart,
     zland,
+    zpart_q,
+    zland_q,
+    pair_v,
+    k_right,
+    k_send1,
+    k_recv1,
+    k_send2,
+    k_recv2,
+    k_hold,
+    k_zpart,
+    k_zland,
     load_sem,
     credit,
     send_sems,
@@ -1732,7 +1791,7 @@
     with_length,
     count,
 ):
-    rows, width = tokens_v.shape
+    rows, width = dres_ref.shape
     seg = rows // slots
     both = wkv_ref.shape[1]
     head_dim = both // 2
@@ -1774,17 +1833,48 @@
     def landing(n, final):
         return lambda way, t: land_v.at[n, way, t - 1] if t < length - 1 else final.at[way]
 
-    up_line = LineSum(links, z, length, line_v.at[0], landing(0, last_v))
-    down_line = LineSum(links, z, length, line_v.at[1], landing(1, down_last))
-    bufs = (left_own, left_out, left_in, right_in, send1, recv1, send2, recv2, hold, zpart, zland)
+    given = [
+        [
+            pltpu.make_async_copy(first_ref_z.at[n, way], land_v.at[n, way, 0], load_sem.at[4 + 2 * n + way])
+            for way in range(2)
+        ]
+        for n in range(2)
+    ]
+    for way, inner in ((0, 1), (1, length - 2)):
+        @pl.when(z == inner)
+        def load_first():
+            given[0][way].start()
+            given[1][way].start()
+
+    up_line = LineSum(links, z, length, line_v.at[0], landing(0, last_v), up_part, given[0])
+    down_line = LineSum(links, z, length, line_v.at[1], landing(1, down_last), down_part, given[1])
+    lanes = ubias_ref.shape[1] // length
+    for level in range(length):
+        ub_part[level] = jnp.broadcast_to(ubias_ref[:, level * lanes : (level + 1) * lanes], ub_part.shape[1:])
+    ubias_line = LineSum(links, z, length, ub_part, lambda way, t: ub_land.at[way, t - 1])
+    bufs = (left_own, left_out, left_in, right_in, send1, recv1, send2, recv2, hold)
     where = (y, c, z, x)
-    mixer = GradSum(links, where, length, width, width, mixed_ref, dmix_v, bufs)
-    query = GradSum(links, where, length, width, width + both, first_ref, right_v, bufs)
+    mixer = GradSum(links, where, length, width, width, mixed_ref, dmix_v, bufs + (zpart, zland))
+    query = GradSum(links, where, length, width, width, dmix_v, right_v, bufs + (zpart_q, zland_q))
+    keyval = GradSum(
+        links,
+        where,
+        length,
+        width,
+        2 * both,
+        dmix_v,
+        pair_v,
+        (left_own, left_out, left_in)
+        + (k_right, k_send1, k_recv1, k_send2, k_recv2, k_hold, k_zpart, k_zland),
+    )
     up_line.clear()
     for way, edge in ((0, 0), (1, length - 1)):
         @pl.when(z == edge)
         def clear_edge():
             zland[way, length - 2] = jnp.zeros(zland.shape[2:], BF)
+            zland_q[way, length - 2] = jnp.zeros(zland_q.shape[2:], BF)
+            k_zland[way, length - 2] = jnp.zeros(k_zland.shape[2:], BF)
+            ub_land[way, length - 2] = jnp.zeros(ub_land.shape[2:], F32)
 
     @pl.when(z == length - 1)
     def clear_hops():
@@ -1810,32 +1900,26 @@
         sent.append(copy)
         return copy
 
-    def hand_over(base):
-        for way, step in ((0, 1), (1, -1)):
-            @pl.when((z + step >= 0) & (z + step < length))
-            def free():
-                pl.semaphore_signal(
-                    credit.at[base + way], inc=1, device_id={"z": z + step}, device_id_type=MESH
-                )
-
-        for way, step in ((0, 1), (1, -1)):
-            @pl.when((z - step >= 0) & (z - step < length))
-            def freed():
-                pl.semaphore_wait(credit.at[base + way], 1)
-
-    load_up.wait()
-    up_line.step(1)
     far = [
         links.copy(red_ref.at[k + 1], far_ref.at[k], device)
         for k, device in enumerate((to_x, to_y, diag))
     ]
-    begin(far[0])
-    begin(far[1])
+    ubias_line.direct(1)
+    ubias_line.direct(2)
+    ubias_line.direct(3)
+    up_line.direct(2)
+    down_line.direct(2)
 
     def to_bf(span):
         dmix_v[span, :] = dres_ref[span, :].astype(BF)
 
     for_rows(rows, to_bf)
+    mixer.share()
+    ubias_line.onward(2)
+    load_up.wait()
+    up_line.onward(2)
+    load_down.wait()
+    down_line.onward(2)
 
     def mix_back(cols, strip_v):
         dmixed_v[:, cols] = dot(dmix_v[...], strip_v[...], ((1,), (1,))).astype(BF)
@@ -1843,6 +1927,7 @@
     mixer_strips.over(mix_back)
     query_strips.start(0)
     query_strips.start(1)
+    mixer.first()
 
     def attend(s, g):
         lanes = pl.ds(pl.multiple_of(g * group * head_dim, group * head_dim), group * head_dim)
@@ -1906,14 +1991,23 @@
             keep_v[s, t] = dkv_v[t, pl.ds(pl.multiple_of(x * seg, seg), seg), :].astype(BF)
             xsend_v[s, t] = dkv_v[t, pl.ds(pl.multiple_of((1 - x) * seg, seg), seg), :].astype(BF)
         x_copies.append(begin(links.copy(xsend_v.at[s], xrecv_v.at[s], to_x)))
-        if s == 0:
-            load_down.wait()
-            down_line.step(1)
-            mixer.share()
-
-    up_line.step(2)
-    mixer.first()
-    begin(far[2])
+    load_tokens = load(tokens_ref, dmixed_v, 8)
+    mixer.second()
+
+    neighbours = ((0, sib), (1, to_y), (2, to_x))
+    for n, device in neighbours:
+        pl.semaphore_signal(credit.at[n], inc=1, device_id=device, device_id_type=MESH)
+    for copy in mixer.sent[:4]:
+        copy.wait_send()
+    load_first = load(first_ref, dmix_v, 9)
+    for n, _ in neighbours:
+        pl.semaphore_wait(credit.at[n], 1)
+    load_first.wait()
+    query.share()
+    query.first()
+    mixer.third(mixer_ref)
+    for n, device in neighbours[1:]:
+        pl.semaphore_signal(credit.at[2 + n], inc=1, device_id=device, device_id_type=MESH)
 
     for copy in x_copies:
         copy.wait_recv()
@@ -1934,88 +2028,64 @@
                 hops[t - 1].start()
             else:
                 for s in range(slots):
-                    right_v[s * seg : (s + 1) * seg, width:] = total[s].astype(BF)
+                    pair_v[s * seg : (s + 1) * seg, :] = total[s].astype(BF)
+
+    keyval.share_right()
+    up_line.direct(3)
+    down_line.direct(3)
+    for t in range(1, length):
+        mixer.line.direct(t)
+    up_line.onward(3)
+    ubias_line.onward(3)
 
     def first_back(cols, strip_v):
-        dfirst_v[:, cols] = dot(right_v[:, :width], strip_v[...], ((1,), (1,))) + dot(
-            right_v[:, width:], wkv_ref[cols, :], ((1,), (1,))
+        dfirst_v[:, cols] = dot(right_v[...], strip_v[...], ((1,), (1,))) + dot(
+            pair_v[...], wkv_ref[cols, :], ((1,), (1,))
         )
 
     query_strips.over(first_back)
-    mixer.second()
-    down_line.step(2)
-
-    mixer.third(mixer_ref)
-    mixer.line.step(1)
-    neighbours = ((0, sib), (1, to_y), (2, to_x))
-    for n, device in neighbours:
-        pl.semaphore_signal(credit.at[n], inc=1, device_id=device, device_id_type=MESH)
-    for n, _ in neighbours:
-        pl.semaphore_wait(credit.at[n], 1)
-    for copy in mixer.sent:
-        copy.wait_send()
-    query.share()
-    query.first()
-
-    vsend_v[0] = jnp.zeros(vsend_v.shape[1:], F32)
+    load_tokens.wait()
+
+    sums_v[...] = jnp.zeros(sums_v.shape, F32)
 
     def first_norm_back(span):
-        unit, rstd = norm_rows(tokens_v[span, :].astype(F32))
+        unit, rstd = norm_rows(dmixed_v[span, :].astype(F32))
         d_first = dfirst_v[span, :]
-        tgrad_ref[span, :] = (
+        dmixed_v[span, :] = (
             dres_ref[span, :] + norm_backward(d_first, unit, rstd, vec_ref[0:1, :])
         ).astype(BF)
-        vsend_v[0, 0:1, :] += jnp.sum(d_first * unit, axis=0, keepdims=True)
-        vsend_v[0, 1:2, :] += jnp.sum(d_first, axis=0, keepdims=True)
-        d_right = right_v[span, :].astype(F32)
-        vsend_v[0, 2:3, :] += jnp.sum(d_right[:, :width], axis=0, keepdims=True)
-        vsend_v[0, 3:4, 0:both] += jnp.sum(d_right[:, width:], axis=0, keepdims=True)
+        sums_v[0:1, :] += jnp.sum(d_first * unit, axis=0, keepdims=True)
+        sums_v[1:2, :] += jnp.sum(d_first, axis=0, keepdims=True)
+        sums_v[2:3, :] += jnp.sum(right_v[span, :].astype(F32), axis=0, keepdims=True)
 
     for_rows(rows, first_norm_back)
-    vsend_v[0, 4:8, :] = vsum_ref[0:4, :]
-    vsend_v[0, 8:9, 0 : ubias_ref.shape[1]] = ubias_ref[...]
-
-    partners = [(sib, 8), (to_x, 8), (to_y, 8)]
-    bit = 1
-    while bit < length:
-        partners.append(({"z": z ^ bit}, 16))
-        bit *= 2
-
-    def exchange(n):
-        device, high = partners[n]
-        copy = begin(links.copy(vsend_v.at[n, pl.ds(0, high)], vrecv_v.at[n, pl.ds(0, high)], device))
-
-        def land():
-            copy.wait_recv()
-            out = vectors_ref if n + 1 == len(partners) else vsend_v.at[n + 1]
-            out[0:high, :] = vsend_v[n, 0:high, :] + vrecv_v[n, 0:high, :]
-            if high == 8:
-                out[8:16, :] = vsend_v[n, 8:16, :]
-
-        return land
-
-    land = exchange(0)
-    up_line.step(3)
-    land()
-    land = exchange(1)
-    mixer.line.step(2)
-    land()
-    land = exchange(2)
+    tgrad_copy = load(dmixed_v, tgrad_ref, 0)
+    sums_v[4:8, :] = vsum_ref[0:4, :]
+
+    devices = 8 * length
+    entries, span = head_dim // devices, width // devices
+    v_sum = jnp.sum(pair_v[:, head_dim:].astype(F32), axis=0, keepdims=True)
+    v_rows = jnp.broadcast_to(v_sum, (8, head_dim)).astype(BF)
+    for j in range(width // 256):
+        entry = lax.broadcasted_iota(jnp.int32, (head_dim, 256), 0)
+        target = lax.broadcasted_iota(jnp.int32, (head_dim, 256), 1) + j * 256
+        spread = (target // span == entry // entries) & (target % span == entry % entries)
+        sums_v[3:4, j * 256 : (j + 1) * 256] = dot(v_rows, jnp.where(spread, 1.0, 0.0).astype(BF))[0:1]
+    keyval.share_sums(sums_v, s_own, s_out, s_in)
+
+    for copy in mixer.sent[4:]:
+        copy.wait_send()
+    for n, _ in neighbours[1:]:
+        pl.semaphore_wait(credit.at[2 + n], 1)
     query.second()
-    land()
-    land = exchange(3)
-    down_line.step(3)
-    for t in range(3, length):
-        mixer.line.step(t)
-    land()
-    land = exchange(4)
-    mixer.finish(mixer_ref)
-    mixer.line.drain()
-    hand_over(3)
+    keyval.first()
+    down_line.onward(3)
     query.third(query_ref)
-    query.line.step(1)
-    land()
-
+    for t in range(1, length):
+        query.line.direct(t)
+    keyval.second()
+
+    tgrad_copy.wait()
     upsum_v = dmixed_v
     up_line.finish(line_v.at[0, z], upsum_v)
     hidden = upsum_v.shape[1] // 2
@@ -2030,6 +2100,15 @@
     up_copies = []
     for flip, device in zip(range(1, 8), plane):
         up_copies.append(begin(links.copy(upsend_v.at[mine ^ flip], uprecv_v.at[flip], device)))
+    for copy in far:
+        begin(copy)
+    keyval.third(keyval_ref)
+    for t in range(1, length):
+        keyval.line.direct(t)
+    for t in range(2, length):
+        mixer.line.onward(t)
+        query.line.onward(t)
+        keyval.line.onward(t)
     out_block = hidden // length
 
     def place_up(flip, ref):
@@ -2039,23 +2118,26 @@
             lanes = pl.ds(pl.multiple_of(base + level * 2 * out_block, out_block), out_block)
             up_ref[:, lanes] = ref[:, level * out_block : (level + 1) * out_block].astype(up_ref.dtype)
 
-    query.line.step(2)
     place_up(0, upsend_v.at[mine])
     for flip, copy in zip(range(1, 8), up_copies):
         copy.wait_recv()
         place_up(flip, uprecv_v.at[flip])
-    for t in range(3, length):
-        query.line.step(t)
+    mixer.finish(mixer_ref)
     for copy in far:
         copy.wait_recv()
     query.finish(query_ref)
+    keyval.finish(keyval_ref)
+    ubias_line.finish(ub_part.at[z], ubias_out)
     for way in range(2):
         @pl.when(down_line.position(way) >= 1)
         def down_landed():
             down_line.copies[way, length - 1].wait_recv()
     for copy in sent:
         copy.wait_send()
+    mixer.line.drain()
+    ubias_line.drain()
     query.drain()
+    keyval.drain()
     up_line.drain()
     down_line.drain()
     for t in range(1, length):
@@ -2065,15 +2147,14 @@
 
 
 def back(lengths, vmem_args, hbm_args, slots, length, with_length):
-    tokens, kv, wkv = vmem_args[0], vmem_args[4], vmem_args[8]
-    rows, width = tokens.shape
+    d_residual, kv, wkv = vmem_args[0], vmem_args[2], vmem_args[6]
+    rows, width = d_residual.shape
     seg = rows // slots
     both = wkv.shape[1]
-    cols = width + both
+    cols = width
     hidden = width // 2
     block = width // (8 * length)
-    stages = 3 + (length - 1).bit_length()
-    count = 96 + 12 * length
+    count = 96 + 16 * length
     hbm = pl.BlockSpec(memory_space=pltpu.HBM)
     vmem = pl.BlockSpec(memory_space=pltpu.VMEM)
     sems = pltpu.SemaphoreType.DMA
@@ -2088,13 +2169,14 @@
         in_specs=[pl.BlockSpec(memory_space=pltpu.SMEM)]
         + [vmem] * len(vmem_args)
         + [hbm] * len(hbm_args),
-        out_specs=[vmem] * 5 + [hbm, hbm],
+        out_specs=[hbm] + [vmem] * 5 + [hbm, hbm],
         out_shape=[
             jax.ShapeDtypeStruct((rows, width), BF),
             jax.ShapeDtypeStruct((block, cols), F32),
+            jax.ShapeDtypeStruct((block, 2 * both), F32),
             jax.ShapeDtypeStruct((block, width), F32),
             jax.ShapeDtypeStruct((block, 8 * hidden), BF),
-            jax.ShapeDtypeStruct((16, width), F32),
+            jax.ShapeDtypeStruct((8, hidden // length), F32),
             jax.ShapeDtypeStruct((3, rows, width), BF),
             jax.ShapeDtypeStruct((2, hidden // length, width), BF),
         ],
@@ -2115,8 +2197,12 @@
             half(2, hidden // length, width),
             half(8, block, hidden),
             half(8, block, hidden),
-            pltpu.VMEM((stages, 16, width), F32),
-            pltpu.VMEM((stages, 16, width), F32),
+            pltpu.VMEM((8, width), F32),
+            half(4, width // 8, 128),
+            half(4, width // 8, 128),
+            half(4, width // 8, 128),
+            pltpu.VMEM((length, 8, hidden // length), F32),
+            pltpu.VMEM((2, length - 1, 8, hidden // length), F32),
             half(4, width // 8, rows),
             half(4, width // 8, rows),
             half(4, width // 8, rows),
@@ -2126,15 +2212,26 @@
             half(2, width // 8, cols // 2),
             half(2, width // 8, cols // 2),
             pltpu.VMEM((width // 8, cols), F32),
+            half(length, block, width),
+            half(2, length - 1, block, width),
             half(length, block, cols),
             half(2, length - 1, block, cols),
-            sems((4,)),
+            half(rows, both),
+            half(rows, both),
+            half(2, 2, width // 8, both),
+            half(2, 2, width // 8, both),
+            half(2, width // 8, both),
+            half(2, width // 8, both),
+            pltpu.VMEM((width // 8, 2 * both), F32),
+            half(length, block, 2 * both),
+            half(2, length - 1, block, 2 * both),
+            sems((10,)),
             pltpu.SemaphoreType.REGULAR((5,)),
             sems((count,)),
             sems((count,)),
         ],
         compiler_params=pltpu.CompilerParams(
-            collective_id=3, has_side_effects=True, vmem_limit_bytes=62 << 20
+            collective_id=3, has_side_effects=True, vmem_limit_bytes=125 << 19
         ),
         cost_estimate=pl.CostEstimate(
             flops=12 * rows * width * width, bytes_accessed=40 << 20, transcendentals=0
@@ -2149,13 +2246,13 @@
     y, c, z, x = where
     rows, width = second.shape
     flat = tokens.reshape(rows, width)
-    d_residual, reduced, down_part, up_part, ubias_part, vsum = feed(
+    d_residual, reduced, down_part, up_part, ubias_part, vsum, ends = feed(
         second, d_down, down_all, up_mine, up_weight, up_bias, residual, vectors, down_weight, length
     )
-    tokens_grad, query_all, mixer_grad, up_grad, sums, far, down_last = back(
+    tokens_grad, query_grad, keyval_all, mixer_grad, up_grad, ubias, far, down_last = back(
         lengths,
-        (flat, d_residual, first, queries, kv_all, mixed, lse, vectors, full_keyval, vsum, ubias_part),
-        (full_query, full_mixer, reduced, down_part.reshape(length, -1, width), up_part),
+        (d_residual, queries, kv_all, mixed, lse, vectors, full_keyval, vsum, ubias_part),
+        (flat, first, full_query, full_mixer, reduced, down_part.reshape(length, -1, width), up_part, ends),
         slots,
         length,
         with_length,
@@ -2167,30 +2264,24 @@
     for term in (reduced[0], far[0], far[1], far[2]):
         output = output + term.astype(F32)
     layer_out = output.astype(BF).reshape(tokens.shape)
-    devices = 8 * length
-    index = (y * 2 + c) * 2 * length + z * 2 + x
-    block = width // devices
-    mine = lax.dynamic_slice_in_dim(sums[:8], index * block, block, 1)
-    head_dim = full_keyval.shape[1] // 2
-    v_block = head_dim // devices
-    vbias = lax.dynamic_slice_in_dim(sums[3], head_dim + index * v_block, v_block, 0)
-    u_block = up_bias.shape[1] // length
-    ubias = lax.dynamic_slice_in_dim(sums[8], z * u_block, u_block, 0)
+    both = full_keyval.shape[1]
+    v_block = both // 2 // (8 * length)
+    mine = keyval_all[:, both : both + 8].T
     return (
         layer_out,
         tokens_grad.reshape(tokens.shape),
         mine[0],
         mine[1],
-        query_all[:, :width],
+        query_grad,
         mine[2],
-        query_all[:, width:],
-        vbias,
+        keyval_all[:, :both],
+        mine[3, :v_block],
         mixer_grad,
         mine[6],
         mine[4],
         mine[5],
         up_grad.astype(F32),
-        ubias,
+        ubias[0],
         down_grad,
         mine[7],
     )
@@ -2229,11 +2320,25 @@
 
     quarter = width // 4
     v_part = value_bias.shape[0]
-    v_place = lax.dynamic_update_slice(jnp.zeros((quarter,), BF), value_bias, (place * v_part,))
-    small = jnp.stack(
-        [norm_gain, norm_shift, query_bias, mixer_bias, ffnorm_gain, ffnorm_shift, down_bias, v_place]
+    lane = jnp.arange(quarter, dtype=jnp.int32) - place * v_part
+    v_wide = jnp.tile(value_bias, quarter // v_part)
+    v_place = jnp.where((lane >= 0) & (lane < v_part), v_wide, jnp.zeros_like(v_wide))
+    small = jnp.concatenate(
+        [
+            v.astype(F32)[None]
+            for v in (
+                norm_gain,
+                norm_shift,
+                query_bias,
+                mixer_bias,
+                ffnorm_gain,
+                ffnorm_shift,
+                down_bias,
+                v_place,
+            )
+        ],
+        axis=0,
     )
-    small = jnp.concatenate([small, jnp.zeros_like(small)], axis=0)
 
     down_mine = pick(down_weight.reshape(length, 2, hidden_block, width), x, 1).reshape(
         hidden_mine, width

time: 469 us -> 432 us (0.921)
  Pallas kernels: 440 us -> 402 us
    pallas_call x1, Pallas kernels: 216 us -> 186 us  [back(): pl.pallas_call(functools.partial(back_kernel, length=length, slots=slots,...]
    pallas_call x1, Pallas kernels: 116 us -> 102 us  [front(): pl.pallas_call(functools.partial(front_kernel, length=length, slots=slots...]
    broadcast_in_dim x2 -> x7, local copies, waits for them, and re-layouts: 0.01 us -> 4.77 us  [body(): v.astype(F32)[None]]
    pallas_call x1, Pallas kernels: 109 us -> 113 us  [feed(): pl.pallas_call(functools.partial(feed_kernel, length=length), in_specs=[h...]
where the time goes in v1:
time: 432 us; the launch traced here: 426 us
  Pallas kernels  402 us (93%)
  local copies, waits for them, and re-layouts  12.8 us (3%)
  other arithmetic  9.67 us (2%)
    pallas_call x1, Pallas kernels, back(): pl.pallas_call(functools.partial(back_kernel, length=length, slots=slots,...  186 us
    pallas_call x1, Pallas kernels, feed(): pl.pallas_call(functools.partial(feed_kernel, length=length), in_specs=[h...  113 us
    pallas_call x1, Pallas kernels, front(): pl.pallas_call(functools.partial(front_kernel, length=length, slots=slots...  102 us

profile of v1, /device:TPU:0, one launch (start us, length us, event | category | flops | bytes accessed | tf_op | source)
XLA Modules:
  0.0 425.6 jit_solution(10427647864322072318)
XLA Ops:
  0.7 0.7 tile.4
  1.3 0.1 tile.10
  1.4 0.7 broadcast_in_dim.37
  2.1 0.7 broadcast_in_dim.38
  2.8 0.7 broadcast_in_dim.39
  3.5 0.7 broadcast_in_dim.40
  4.1 0.7 broadcast_in_dim.41
  4.8 0.7 broadcast_in_dim.42
  5.5 0.7 broadcast_in_dim.43
  6.2 0.6 concatenate.6.smalls_ref
  6.8 0.0 copy-start.7
  6.8 102.4 %shard_map.288 = (bf16[256,2048]{1,0:T(8,128)(2,1)}, f32[256,2048]{1,0:T(8,128)}, bf16[256,2048]{1,0:T(8,128)(2,1)}, bf16[256,2048]{1,0:T(8,128)(2,1)}, bf16[2,4...) custom-call(s32[2]{0:T(128)} %lengths_ref.3, ...), custom_call_target="tpu_custom_call" | custom-call | flops 6442450944 | bytes 41943040 | tf_op jit(solution)/shard_map/pallas_call | solution.py:1001
  109.3 0.0 copy-done.7
  109.3 0.6 convert.13.ubias_ref
  109.9 113.3 %shard_map.289 = (f32[256,2048]{1,0:T(8,128)}, bf16[4,256,2048]{2,1,0:T(8,128)(2,1)}, bf16[1024,2048]{1,0:T(8,128)(2,1)}, bf16[4,256,2048]{2,1,0:T(8,128)(2,1)},...) custom-call(bf16[256,2048]{1,0:T(8,128)(2,1)} %get-tuple-element.46.second_ref, ...), custom_call_target="tpu_custom_call" | custom-call | flops 51539607552 | bytes 41943040 | tf_op jit(solution)/shard_map/pallas_call | solution.py:1394
  223.2 186.3 %shard_map.290 = (bf16[256,2048]{1,0:T(8,128)(2,1)}, f32[64,2048]{1,0:T(8,128)}, f32[64,512]{1,0:T(8,128)}, f32[64,2048]{1,0:T(8,128)}, bf16[64,8192]{1,0:T(8,12...) custom-call(s32[2]{0:T(128)} %lengths_ref.3, ...), custom_call_target="tpu_custom_call" | custom-call | flops 12884901888 | bytes 41943040 | tf_op jit(solution)/shard_map/pallas_call | solution.py:2165
  409.5 0.0 copy-start.2
  409.5 0.0 copy-start.1
  409.5 3.9 add_bitcast_fusion
  413.4 0.0 copy-start
  413.4 0.0 copy-done.2
  413.4 1.5 convert_element_type.73
  414.8 1.1 slice.54
  415.9 0.0 copy-done.1
  415.9 0.1 copy-done
  416.0 0.0 copy-start.6
  416.0 0.0 copy-start.3
  416.0 3.1 fusion
  419.2 0.0 copy-start.5
  419.2 0.0 copy-start.4
  419.2 0.0 copy-done.6
  419.2 0.6 slice.63
  419.8 0.8 slice_reduce_fusion
  420.6 0.7 slice_reduce_fusion.7
  421.3 1.3 slice.68
  422.6 0.0 copy-done.3
  422.6 1.0 copy.36
  423.6 0.0 copy-done.5
  423.6 0.8 copy.37
  424.4 0.0 copy-done.4
  424.4 0.8 copy.38
  (5 shorter events, 0.1 us)
Async XLA Ops:
  6.8 102.5 %copy-start.7 = (bf16[2048]{0:T(1024)(128)(2,1)S(1)}, bf16[2048]{0:T(1024)(128)(2,1)}, u32[]{:S(2)}) copy-start(bf16[2048]{0:T(1024)(128)(2,1)} %param.31) | copy-start | bytes 12292
  409.5 3.9 copy-start.2
  409.5 6.4 %copy-start.1 = (f32[256,2048]{1,0:T(8,128)S(1)}, f32[256,2048]{1,0:T(8,128)}, u32[]{:S(2)}) copy-start(f32[256,2048]{1,0:T(8,128)} %get-tuple-element.44.residual_ref) | copy-start | bytes 6291460
  413.4 2.6 copy-start
  416.0 3.1 copy-start.6
  416.0 6.6 %copy-start.3 = (bf16[256,2048]{1,0:T(8,128)(2,1)S(1)}, bf16[256,2048]{1,0:T(8,128)(2,1)}, u32[]{:S(2)}) copy-start(bf16[256,2048]{1,0:T(8,128)(2,1)} %get-tuple-element.65) | copy-start | bytes 3145732
  419.2 4.4 %copy-start.5 = (f32[64,2048]{1,0:T(8,128)S(1)}, f32[64,2048]{1,0:T(8,128)}, u32[]{:S(2)}) copy-start(f32[64,2048]{1,0:T(8,128)} %get-tuple-element.99) | copy-start | bytes 1572868
  419.2 5.2 %copy-start.4 = (f32[64,2048]{1,0:T(8,128)S(1)}, f32[64,2048]{1,0:T(8,128)}, u32[]{:S(2)}) copy-start(f32[64,2048]{1,0:T(8,128)} %get-tuple-element.103) | copy-start | bytes 1572868

commit v2 on v1

--- a/solution.py
+++ b/solution.py
@@ -658,7 +658,14 @@
 def front_kernel(
     lengths_ref,
     tokens_v,
-    smalls_ref,
+    *refs,
+    length,
+    slots,
+    with_length,
+    aligned,
+):
+    smalls, refs = refs[:8], refs[8:]
+    (
     kvw_ref,
     qw_ref,
     mw_ref,
@@ -693,12 +700,8 @@
     uz_recv,
     c_send,
     c_recv,
-    *,
-    length,
-    slots,
-    with_length,
-    aligned,
-):
+    smalls_ref,
+    ) = refs
     rows, width = tokens_v.shape
     seg = rows // slots
     head_dim = kvw_ref.shape[1] // 2
@@ -718,6 +721,8 @@
     locals_ = [query_w.own(local_sem.at[0]), mixer_w.own(local_sem.at[1])]
     kv_rows = pl.ds(pl.multiple_of(place * quarter, quarter), quarter)
     locals_.append(pltpu.make_async_copy(kvw_ref, wkv_v.at[kv_rows], local_sem.at[2]))
+    for row, vector in enumerate(smalls):
+        smalls_ref[row : row + 1, :] = vector[...].astype(F32).reshape(1, -1)
     locals_.append(pltpu.make_async_copy(smalls_ref, smalls_v.at[place], local_sem.at[3]))
     for copy in locals_:
         copy.start()
@@ -1002,7 +1007,7 @@
         functools.partial(
             front_kernel, length=length, slots=slots, with_length=with_length, aligned=aligned
         ),
-        in_specs=[pl.BlockSpec(memory_space=pltpu.SMEM), vmem, hbm, hbm, hbm, hbm, hbm, hbm],
+        in_specs=[pl.BlockSpec(memory_space=pltpu.SMEM), vmem] + [vmem] * 8 + [hbm] * 5,
         out_specs=[vmem] * 8 + [hbm, hbm, vmem, hbm, hbm],
         out_shape=[
             jax.ShapeDtypeStruct((rows, width), BF),
@@ -1036,6 +1041,7 @@
             sems((2, length)),
             sems((8,)),
             sems((8,)),
+            pltpu.VMEM((8, width // 4), F32),
         ],
         compiler_params=pltpu.CompilerParams(
             collective_id=2, has_side_effects=True, vmem_limit_bytes=60 << 20
@@ -1043,7 +1049,7 @@
         cost_estimate=pl.CostEstimate(
             flops=6 * rows * width * width, bytes_accessed=40 << 20, transcendentals=0
         ),
-    )(lengths, tokens, smalls, kvw, qw, mw, up, cot)
+    )(lengths, tokens, *smalls, kvw, qw, mw, up, cot)
 
 
 def feed_kernel(
@@ -1581,7 +1587,7 @@
         for core, target in ((1 - self.c, self.left_out), (self.c, self.left_own)):
             for y_part in range(2):
                 lanes = pl.ds(pl.multiple_of((y_part * 2 + core) * quarter, quarter), quarter)
-                turned = self.left[:, lanes].astype(F32).T.astype(BF)
+                turned = self.left[:, lanes].T
                 for x_part in range(2):
                     for level in range(self.length):
                         start = (level * 2 + x_part) * block
@@ -2323,22 +2329,19 @@
     lane = jnp.arange(quarter, dtype=jnp.int32) - place * v_part
     v_wide = jnp.tile(value_bias, quarter // v_part)
     v_place = jnp.where((lane >= 0) & (lane < v_part), v_wide, jnp.zeros_like(v_wide))
-    small = jnp.concatenate(
-        [
-            v.astype(F32)[None]
-            for v in (
-                norm_gain,
-                norm_shift,
-                query_bias,
-                mixer_bias,
-                ffnorm_gain,
-                ffnorm_shift,
-                down_bias,
-                v_place,
-            )
-        ],
-        axis=0,
-    )
+    small = [
+        v
+        for v in (
+            norm_gain,
+            norm_shift,
+            query_bias,
+            mixer_bias,
+            ffnorm_gain,
+            ffnorm_shift,
+            down_bias,
+            v_place,
+        )
+    ]
 
     down_mine = pick(down_weight.reshape(length, 2, hidden_block, width), x, 1).reshape(
         hidden_mine, width

time: 432 us -> 427 us (0.988)
  local copies, waits for them, and re-layouts: 12.8 us -> 7.96 us
    broadcast_in_dim x7 -> x0, local copies, waits for them, and re-layouts: 4.77 us -> none  [body(): v.astype(F32)[None]]
where the time goes in v2:
time: 427 us; the launch traced here: 421 us
  Pallas kernels  402 us (94%)
  other arithmetic  9.61 us (2%)
  local copies, waits for them, and re-layouts  7.96 us (2%)
    pallas_call x1, Pallas kernels, back(): pl.pallas_call(functools.partial(back_kernel, length=length, slots=slots,...  186 us
    pallas_call x1, Pallas kernels, feed(): pl.pallas_call(functools.partial(feed_kernel, length=length), in_specs=[h...  114 us
    pallas_call x1, Pallas kernels, front(): pl.pallas_call(functools.partial(front_kernel, length=length, slots=slots...  102 us

profile of v2, /device:TPU:0, one launch (start us, length us, event | category | flops | bytes accessed | tf_op | source)
XLA Modules:
  0.0 420.9 jit_solution(15755279593508953960)
XLA Ops:
  0.7 0.7 tile.4
  1.3 0.1 tile.10
  1.4 0.6 fusion.4.refs_7_
  2.0 0.0 copy-start.7
  2.0 102.4 %shard_map.288 = (bf16[256,2048]{1,0:T(8,128)(2,1)}, f32[256,2048]{1,0:T(8,128)}, bf16[256,2048]{1,0:T(8,128)(2,1)}, bf16[256,2048]{1,0:T(8,128)(2,1)}, bf16[2,4...) custom-call(s32[2]{0:T(128)} %lengths_ref.3, ...), custom_call_target="tpu_custom_call" | custom-call | flops 6442450944 | bytes 41943040 | tf_op jit(solution)/shard_map/pallas_call | solution.py:1006
  104.3 0.0 copy-done.7
  104.4 0.6 convert.5.ubias_ref
  105.0 113.5 %shard_map.289 = (f32[256,2048]{1,0:T(8,128)}, bf16[4,256,2048]{2,1,0:T(8,128)(2,1)}, bf16[1024,2048]{1,0:T(8,128)(2,1)}, bf16[4,256,2048]{2,1,0:T(8,128)(2,1)},...) custom-call(bf16[256,2048]{1,0:T(8,128)(2,1)} %get-tuple-element.46.second_ref, ...), custom_call_target="tpu_custom_call" | custom-call | flops 51539607552 | bytes 41943040 | tf_op jit(solution)/shard_map/pallas_call | solution.py:1400
  218.5 186.3 %shard_map.290 = (bf16[256,2048]{1,0:T(8,128)(2,1)}, f32[64,2048]{1,0:T(8,128)}, f32[64,512]{1,0:T(8,128)}, f32[64,2048]{1,0:T(8,128)}, bf16[64,8192]{1,0:T(8,12...) custom-call(s32[2]{0:T(128)} %lengths_ref.3, ...), custom_call_target="tpu_custom_call" | custom-call | flops 12884901888 | bytes 41943040 | tf_op jit(solution)/shard_map/pallas_call | solution.py:2171
  404.8 0.0 copy-start.2
  404.8 0.0 copy-start.1
  404.8 3.9 add_bitcast_fusion
  408.7 0.0 copy-start
  408.7 0.0 copy-done.2
  408.7 1.5 convert_element_type.58
  410.1 1.1 slice.54
  411.2 0.0 copy-done.1
  411.2 0.1 copy-done
  411.3 0.0 copy-start.6
  411.3 0.0 copy-start.3
  411.3 3.1 fusion
  414.4 0.0 copy-start.5
  414.4 0.0 copy-start.4
  414.4 0.0 copy-done.6
  414.4 0.6 slice.63
  415.1 0.8 slice_reduce_fusion
  415.9 0.7 slice_reduce_fusion.7
  416.6 1.3 slice.68
  417.9 0.0 copy-done.3
  417.9 1.0 copy.36
  418.8 0.0 copy-done.5
  418.8 0.8 copy.37
  419.6 0.0 copy-done.4
  419.6 0.8 copy.38
  (3 shorter events, 0.0 us)
Async XLA Ops:
  2.0 102.4 %copy-start.7 = (bf16[2048]{0:T(1024)(128)(2,1)S(1)}, bf16[2048]{0:T(1024)(128)(2,1)}, u32[]{:S(2)}) copy-start(bf16[2048]{0:T(1024)(128)(2,1)} %param.31) | copy-start | bytes 12292
  404.8 3.9 copy-start.2
  404.8 6.4 %copy-start.1 = (f32[256,2048]{1,0:T(8,128)S(1)}, f32[256,2048]{1,0:T(8,128)}, u32[]{:S(2)}) copy-start(f32[256,2048]{1,0:T(8,128)} %get-tuple-element.44.residual_ref) | copy-start | bytes 6291460
  408.7 2.6 copy-start
  411.3 3.1 copy-start.6
  411.3 6.6 %copy-start.3 = (bf16[256,2048]{1,0:T(8,128)(2,1)S(1)}, bf16[256,2048]{1,0:T(8,128)(2,1)}, u32[]{:S(2)}) copy-start(bf16[256,2048]{1,0:T(8,128)(2,1)} %get-tuple-element.65) | copy-start | bytes 3145732
  414.4 4.4 %copy-start.5 = (f32[64,2048]{1,0:T(8,128)S(1)}, f32[64,2048]{1,0:T(8,128)}, u32[]{:S(2)}) copy-start(f32[64,2048]{1,0:T(8,128)} %get-tuple-element.99) | copy-start | bytes 1572868
  414.4 5.2 %copy-start.4 = (f32[64,2048]{1,0:T(8,128)S(1)}, f32[64,2048]{1,0:T(8,128)}, u32[]{:S(2)}) copy-start(f32[64,2048]{1,0:T(8,128)} %get-tuple-element.103) | copy-start | bytes 1572868
